TPU v7x, 32 devices: a whole 2x2x4 slice. The times are simulated.
32 devices in a mesh: feat: 8 (over y, x, core), grp: 4 (over z).
Axes of the slice: x: 2, y: 2, z: 4, core: 2. Of those that a mesh axis runs over, the one named last changes fastest.
Arguments:
- x_feat: bfloat16 [4, 128, 8192], P('grp', 'feat'), may hold values from -6 to 6
- place: int32 [4, 64], P('grp'), may hold values from 0 to 63, each once within a row
- adj_one: bfloat16 [4, 64, 4, 128, 128], P('grp'), may hold values from -0.25 to 0.25
- cols_one: int32 [4, 64, 4], P('grp'), may hold values from 0 to 63
- count_one: int32 [4, 64], P('grp'), may hold values from 1 to 4
- w_one: bfloat16 [2, 128, 256], P(None, 'feat'), may hold values from -0.5 to 0.5
- bias_one: bfloat16 [256], replicated, may hold values from -3 to 3
- adj_two: bfloat16 [4, 64, 8, 128, 128], P('grp', 'feat'), may hold values from -0.1875 to 0.1875
- cols_two: int32 [4, 64, 8], P('grp', 'feat'), may hold values from 0 to 63, as said below
- count_two: int32 [4, 64], P('grp', 'feat'), may hold values from 1 to 8
- w_two: bfloat16 [2, 256, 256], replicated, may hold values from -0.375 to 0.375
- cotangent: bfloat16 [4, 8192, 256], P('grp', 'feat'), may hold values from -0.03125 to 0.03125
Outputs:
- layer_out: bfloat16 [4, 8192, 256], P('grp', 'feat')
- grad_one: float32 [2, 128, 256], P(None, 'feat')
Inputs may be any that keep to these rules, and one draw needn't show every extreme that they name: `cols_two`: among the entries of the 8 row tiles of one device, at most 8 name tiles of any one owner (owner = value // 8), and no two name the same tile; in every group some owner is named exactly 8 times by every device. `place`: each row is a permutation of the group's row tiles.
All inputs are finite; a program needn't handle non-finite values.
Results may differ from a plain program's by a relative error of at most 0.0056.
Values may be sent and summed in bfloat16 or wider, within the bound.
No kernel may reach another device: no remote copies, remote signals or barrier semaphores. Data moves between devices by JAX's collectives and lax.ppermute only.
A program may use at most 128 MiB of HBM per device.

v0:
```python
import jax
import jax.numpy as jnp
from jax import lax
from jax.sharding import PartitionSpec as P


def project(features, weight):
    return lax.dot_general(
        features, weight, (((0,), (0,)), ((), ())), preferred_element_type=jnp.float32
    )


def body(
    x_feat,
    place,
    adj_one,
    cols_one,
    count_one,
    w_one,
    bias_one,
    adj_two,
    cols_two,
    count_two,
    w_two,
    cotangent,
):
    x_local = x_feat[0]
    feat_dev, group_rows = x_local.shape
    tile_size = adj_one.shape[-1]
    group_tiles = place.shape[1]
    fan_one = adj_one.shape[2]
    own_tiles = adj_two.shape[1]
    fan_two = adj_two.shape[2]
    hidden_width = w_two.shape[-1]
    feat_count = lax.axis_size("feat")
    capacity = max(2, (own_tiles * fan_two + feat_count - 1) // feat_count)
    x_tiles = x_local.reshape(feat_dev, group_tiles, tile_size)
    live_one = (jnp.arange(fan_one)[None, :] < count_one[0][:, None]).astype(jnp.bfloat16)
    windows = x_tiles[:, cols_one[0]] * live_one[None, :, :, None]
    agg_local = jnp.einsum(
        "ftkj,tkij->fti", windows, adj_one[0], preferred_element_type=jnp.float32
    ).astype(jnp.bfloat16)
    inverse = (
        jnp.zeros((group_tiles,), jnp.int32)
        .at[place[0]]
        .set(jnp.arange(group_tiles, dtype=jnp.int32))
    )
    x_placed = x_tiles[:, inverse].reshape(feat_dev, group_rows)
    agg_placed = agg_local[:, inverse].reshape(feat_dev, group_rows)
    bias_row = bias_one.astype(jnp.float32)
    x_own, agg_own = (
        lax.all_to_all(x_placed, "feat", split_axis=1, concat_axis=0, tiled=True),
        lax.all_to_all(agg_placed, "feat", split_axis=1, concat_axis=0, tiled=True),
    )
    full_weight = lax.all_gather(w_one, "feat", axis=1, tiled=True)
    z_one = project(x_own, full_weight[0]) + project(agg_own, full_weight[1]) + bias_row
    h_one = jax.nn.silu(z_one).astype(jnp.bfloat16)
    tiles_mine = h_one.reshape(own_tiles, tile_size, hidden_width)
    flat_cols = cols_two[0].reshape(-1)
    entries = flat_cols.shape[0]
    owners = flat_cols // own_tiles
    slot_ids = flat_cols % own_tiles
    entry_index = jnp.arange(entries)
    earlier = (owners[:, None] == owners[None, :]) & (entry_index[:, None] > entry_index[None, :])
    target = owners * capacity + jnp.sum(earlier.astype(jnp.int32), axis=1)
    chosen = (target[:, None] == jnp.arange(feat_count * capacity)[None, :]).astype(jnp.int32)
    request = jnp.sum(chosen * slot_ids[:, None], axis=0).reshape(feat_count, capacity)
    received = lax.all_to_all(request, "feat", split_axis=0, concat_axis=0, tiled=True)
    picked = tiles_mine[received]
    fetched = lax.all_to_all(picked, "feat", split_axis=0, concat_axis=0, tiled=True)
    neighbour_rows = fetched.reshape(feat_count * capacity, tile_size, hidden_width)[target]
    neighbour_rows = neighbour_rows.reshape(own_tiles, fan_two, tile_size, hidden_width)
    live_two = (jnp.arange(fan_two)[None, :] < count_two[0][:, None]).astype(jnp.bfloat16)
    adj_live = adj_two[0] * live_two[:, :, None, None]
    agg_two = jnp.einsum(
        "tkij,tkjh->tih", adj_live, neighbour_rows, preferred_element_type=jnp.float32
    )
    agg_two = agg_two.astype(jnp.bfloat16).reshape(own_tiles * tile_size, hidden_width)
    z_two = jnp.dot(h_one, w_two[0], preferred_element_type=jnp.float32)
    layer_out = (z_two + jnp.dot(agg_two, w_two[1], preferred_element_type=jnp.float32)).astype(
        jnp.bfloat16
    )
    cot_rows = cotangent[0]
    back_self = lax.dot_general(
        cot_rows, w_two[0], (((1,), (1,)), ((), ())), preferred_element_type=jnp.float32
    )
    back_neigh = lax.dot_general(
        cot_rows, w_two[1], (((1,), (1,)), ((), ())), preferred_element_type=jnp.float32
    )
    back_neigh = back_neigh.astype(jnp.bfloat16).reshape(own_tiles, tile_size, hidden_width)
    sent_terms = jnp.einsum(
        "tkji,tjh->tkih", adj_live, back_neigh, preferred_element_type=jnp.float32
    )
    sent_terms = sent_terms.astype(jnp.bfloat16).reshape(entries, tile_size, hidden_width)
    outgoing = (
        jnp.zeros((feat_count * capacity, tile_size, hidden_width), jnp.bfloat16)
        .at[target]
        .set(sent_terms)
    )
    outgoing = outgoing.reshape(feat_count, capacity, tile_size, hidden_width)
    incoming = lax.all_to_all(outgoing, "feat", split_axis=0, concat_axis=0, tiled=True)
    selector = (received.reshape(-1)[None, :] == jnp.arange(own_tiles)[:, None]).astype(
        jnp.bfloat16
    )
    returned_sum = jnp.dot(
        selector,
        incoming.reshape(feat_count * capacity, tile_size * hidden_width),
        preferred_element_type=jnp.float32,
    )
    d_hidden = back_self + returned_sum.reshape(own_tiles * tile_size, hidden_width)
    sigmoid_z = jax.nn.sigmoid(z_one)
    d_pre = (d_hidden * sigmoid_z * (1.0 + z_one * (1.0 - sigmoid_z))).astype(jnp.bfloat16)
    local_grads = jnp.stack(
        [
            jnp.dot(x_own, d_pre, preferred_element_type=jnp.float32),
            jnp.dot(agg_own, d_pre, preferred_element_type=jnp.float32),
        ]
    )
    shares = lax.psum_scatter(local_grads, "feat", scatter_dimension=1, tiled=True)
    grad_sum = lax.psum(shares, "grp")
    return (layer_out[None], grad_sum)


def solution(mesh):
    in_specs = (
        P("grp", "feat", None),
        P("grp", None),
        P("grp", None, None, None, None),
        P("grp", None, None),
        P("grp", None),
        P(None, "feat", None),
        P(),
        P("grp", "feat", None, None, None),
        P("grp", "feat", None),
        P("grp", "feat"),
        P(),
        P("grp", "feat", None),
    )
    out_specs = (P("grp", "feat", None), P(None, "feat", None))
    return jax.shard_map(body, mesh=mesh, in_specs=in_specs, out_specs=out_specs, check_vma=False)
```

profile of v0, /device:TPU:0, one launch (start us, length us, event | category | flops | bytes accessed | tf_op | source)
XLA Modules:
  0.0 218.0 jit_solution(943387714860465447)
XLA Ops:
  7.2 0.0 copy-start
  7.2 0.8 reshape_squeeze.9
  8.0 0.2 convert_reduce_fusion
  8.2 0.1 select_reduce_fusion
  8.3 0.7 all_to_all.50
  9.0 5.2 %all-to-all-start.2 = ((s32[8,1,8]{2,1,0:T(1,128)}), s32[8,1,8]{2,1,0:T(1,128)S(1)}, u32[]{:S(2)}, u32[]{:S(2)}) async-start(s32[8,1,8]{2,1,0:T(1,128)} %bitcast.22), calls=%async_computation.2 | async-start | bytes 8192 | tf_op jit(solution)/shard_map/all_to_all | solution.py:68
  14.2 1.0 copy.50
  15.2 0.2 copy.37
  15.3 0.7 fusion.42
  16.0 0.8 scatter_custom_fusion
  16.8 0.7 compare_select_fusion.1
  17.5 0.1 copy.40
  17.6 0.1 reshape.358
  17.7 0.6 gather_fusion
  18.4 0.8 gather_fusion.1
  19.2 0.7 fusion.37
  19.9 6.4 %fusion.17 = bf16[16,64,128]{2,0,1:T(8,128)(2,1)} fusion(bf16[1,64,4,128,128]{4,3,2,1,0:T(8,128)(2,1)} %param.14, bf16[64,4,16,128]{3,2,1,0:T(8,128)(2,1)S(1)} %bitcast.126, bf16[64,4]{1,0:T(8,128)(2,1)S(1)} %fusion.37), kind=kOutput, calls=%fused_computation.26 | convolution fusion | flops 134873088 | bytes 9699840 | tf_op jit(solution)/shard_map/ftkj,tkij->fti/dot_general | solution.py:40
  26.4 0.1 copy.38
  26.4 0.1 all_to_all.42
  26.6 0.9 copy.39
  27.4 0.0 all-to-all-done.2
  27.4 4.2 %all-to-all-start = ((bf16[16,8,1024]{2,0,1:T(8,128)(2,1)}), bf16[16,8,1024]{2,0,1:T(8,128)(2,1)S(1)}, u32[]{:S(2)}, u32[]{:S(2)}) async-start(bf16[16,8,1024]{2,0,1:T(8,128)(2,1)} %copy.39), calls=%async_computation | async-start | bytes 524288 | tf_op jit(solution)/shard_map/all_to_all | solution.py:52
  31.6 0.0 copy-done
  31.6 1.2 convolution_convert_fusion.1
  32.9 2.3 %gather_fusion.2 = bf16[64,16,128]{2,1,0:T(8,128)(2,1)} fusion(bf16[16,64,128]{2,0,1:T(8,128)(2,1)} %fusion.17, s32[1024]{0:T(1024)S(1)} %pad_clamp_fusion.3), kind=kCustom, calls=%fused_computation.2 | custom fusion | bytes 524544 | tf_op jit(solution)/shard_map/gather | solution.py:49
  35.1 1.7 copy.42
  36.8 1.8 all_to_all.46
  38.6 1.8 copy.43
  40.4 0.0 copy-done.6
  40.4 0.1 fusion.39
  40.5 0.0 all-to-all-done
  40.5 4.2 %all-to-all-start.1 = ((bf16[16,8,1024]{2,0,1:T(8,128)(2,1)}), bf16[16,8,1024]{2,0,1:T(8,128)(2,1)}, u32[]{:S(2)}, u32[]{:S(2)}) async-start(bf16[16,8,1024]{2,0,1:T(8,128)(2,1)} %copy.43), calls=%async_computation.1 | async-start | bytes 524288 | tf_op jit(solution)/shard_map/all_to_all | solution.py:53
  44.7 3.9 %convolution_convert_fusion = bf16[8,8,128,256]{3,2,1,0:T(8,128)(2,1)} fusion(bf16[8,128,256,1]{2,1,3,0:T(8,128)(2,1)S(1)} %bitcast.130, bf16[1,8,8,128,128]{4,3,2,1,0:T(8,128)(2,1)S(1)} %copy-done.1, bf16[8,8]{1,0:T(8,128)(2,1)S(1)} %fusion.39), kind=kOutput, calls=%fused_computation.9 | convolution fusion | flops 540016640 | bytes 6815872 | tf_op jit(solution)/shard_map/tkji,tjh->tkih/dot_general | solution.py:91
  48.6 0.1 reshape_squeeze.10
  48.7 2.4 %broadcast_in_dim.8 = bf16[64,128,256]{2,1,0:T(8,128)(2,1)} broadcast(bf16[]{:T(256)} %constant.43.clone.1), dimensions={} | broadcast | bytes 4194306 | tf_op jit(solution)/shard_map/broadcast_in_dim | solution.py:96
  51.2 12.0 %scatter_fusion = bf16[64,128,256]{2,1,0:T(8,128)(2,1)} fusion(bf16[64,128,256]{2,1,0:T(8,128)(2,1)} %broadcast_in_dim.8, s32[64]{0:T(128)S(1)} %fusion.43, bf16[64,128,256]{2,1,0:T(8,128)(2,1)} %bitcast.123), kind=kCustom, calls=%fused_computation.6 | custom fusion | bytes 12583168 | tf_op jit(solution)/shard_map/scatter | solution.py:98
  63.1 0.0 all-to-all-done.1
  63.2 4.7 %all-to-all-start.4 = ((bf16[8,8,128,256]{3,2,1,0:T(8,128)(2,1)}), bf16[8,8,128,256]{3,2,1,0:T(8,128)(2,1)}, u32[]{:S(2)}, u32[]{:S(2)}) async-start(bf16[8,8,128,256]{3,2,1,0:T(8,128)(2,1)} %bitcast.122), calls=%async_computation.4 | async-start | bytes 8388608 | tf_op jit(solution)/shard_map/all_to_all | solution.py:101
  67.9 52.5 %all_gather.3 = bf16[2,128,256]{2,1,0:T(8,128)(2,1)S(1)} all-gather(bf16[2,16,256]{2,1,0:T(8,128)(2,1)S(1)} %copy-done.4), channel_id=1, replica_groups=mesh['feat'=8,'grp'=4] {'feat'}, dimensions={1}, use_global_device_ids=true | all-gather | bytes 147456 | tf_op jit(solution)/shard_map/all_gather | solution.py:55
  120.4 0.1 reshape.374
  120.5 0.3 fusion.36
  120.8 2.4 %multiply_convert_fusion = (bf16[1024,256]{1,0:T(8,128)(2,1)S(1)}, f32[1024,256]{1,0:T(8,128)}) fusion(f32[256]{0:T(256)S(1)} %convert_element_type.49, f32[1024,256]{1,0:T(8,128)S(1)} %fusion.36, bf16[128,1024]{1,0:T(8,128)(2,1)} %bitcast.16, bf16[2,128,256]{2,1,0:T(8,128)(2,1)S(1)} %all_gather.3), kind=kOutput, calls=%fused_computation.33 | convolution fusion | flops 68943872 | bytes 2950144 | tf_op jit(solution)/shard_map/dot_general | solution.py:8
  123.2 2.8 %gather_fusion.3 = bf16[64,128,256]{2,1,0:T(8,128)(2,1)} fusion(bf16[8,128,256]{2,1,0:T(8,128)(2,1)S(1)} %bitcast.121, s32[1024]{0:T(1024)S(1)} %pad_clamp_fusion.1), kind=kCustom, calls=%fused_computation.3 | custom fusion | bytes 8388864 | tf_op jit(solution)/shard_map/gather | solution.py:69
  126.0 0.0 all-to-all-done.4
  126.0 4.7 %all-to-all-start.3 = ((bf16[8,8,128,256]{3,2,1,0:T(8,128)(2,1)}), bf16[8,8,128,256]{3,2,1,0:T(8,128)(2,1)}, u32[]{:S(2)}, u32[]{:S(2)}) async-start(bf16[8,8,128,256]{3,2,1,0:T(8,128)(2,1)} %bitcast.125), calls=%async_computation.3 | async-start | bytes 8388608 | tf_op jit(solution)/shard_map/all_to_all | solution.py:70
  130.7 0.2 reduce-scatter.2.cloned.1.call-start
  131.0 0.5 broadcast.296
  131.5 0.7 reduce.3
  132.1 0.1 eq.46
  132.2 0.3 fusion.30
  132.5 4.8 %copy.51 = bf16[8,8,128,256]{3,1,2,0:T(8,128)(2,1)S(1)} copy(bf16[8,8,128,256]{3,2,1,0:T(8,128)(2,1)} %all-to-all-done.4) | data formatting | bytes 8388608
  137.3 0.0 copy-start.3
  137.3 0.7 fusion.40
  137.9 1.2 reshape.347
  139.1 2.1 fusion.9
  141.2 1.2 convolution_bitcast_fusion
  142.4 0.2 convolution_bitcast_fusion.1
  142.7 0.7 pad_maximum_fusion
  143.4 0.0 reduce-scatter.2.cloned.1.call-update
  143.4 37.5 %all-to-all-done.3 = bf16[8,8,128,256]{3,2,1,0:T(8,128)(2,1)} async-done(((bf16[8,8,128,256]{3,2,1,0:T(8,128)(2,1)}), bf16[8,8,128,256]{3,2,1,0:T(8,128)(2,1)}, u32[]{:S(2)}, u32[]{:S(2)}) %all-to-all-start.3) | async-done | bytes 4194336 | tf_op jit(solution)/shard_map/all_to_all | solution.py:70
  180.9 5.0 %gather_fusion.4 = bf16[64,128,256]{2,1,0:T(8,128)(2,1)} fusion(bf16[64,128,256]{2,1,0:T(8,128)(2,1)} %bitcast.25, s32[1024]{0:T(1024)S(1)} %pad_clamp_fusion), kind=kCustom, calls=%fused_computation.4 | custom fusion | bytes 8388864 | tf_op jit(solution)/shard_map/gather | solution.py:71
  185.9 3.7 %fusion.7 = bf16[8,128,256]{2,1,0:T(8,128)(2,1)S(1)} fusion(bf16[8,8,128,256]{3,2,1,0:T(8,128)(2,1)} %bitcast.127, bf16[1,8,8,128,128]{4,3,2,1,0:T(8,128)(2,1)} %param.19, bf16[8,8]{1,0:T(8,128)(2,1)S(1)} %fusion.39), kind=kOutput, calls=%fused_computation.19 | convolution fusion | flops 538181632 | bytes 6815872 | tf_op jit(solution)/shard_map/tkij,tkjh->tih/dot_general | solution.py:75
  189.6 1.1 fusion.10
  190.7 20.5 %psum.7 = f32[2,16,256]{2,1,0:T(8,128)} all-reduce(f32[2,16,256]{2,1,0:T(8,128)} %reduce-scatter.2.cloned.1.call-done), channel_id=1, replica_groups=mesh['feat'=8,'grp'=4] {'grp'}, use_global_device_ids=true, to_apply=%region_5.6 | all-reduce | flops 8192 | bytes 65536 | tf_op jit(solution)/shard_map/psum | solution.py:120
  (24 shorter events, 0.1 us)
Async XLA Ops:
  7.2 24.4 %copy-start = (bf16[1,1024,256]{2,1,0:T(8,128)(2,1)S(1)}, bf16[1,1024,256]{2,1,0:T(8,128)(2,1)}, u32[]{:S(2)}) copy-start(bf16[1,1024,256]{2,1,0:T(8,128)(2,1)} %param.23) | copy-start | bytes 1572868
  9.0 18.4 %all-to-all-start.2 = ((s32[8,1,8]{2,1,0:T(1,128)}), s32[8,1,8]{2,1,0:T(1,128)S(1)}, u32[]{:S(2)}, u32[]{:S(2)}) async-start(s32[8,1,8]{2,1,0:T(1,128)} %bitcast.22), calls=%async_computation.2 | async-start | bytes 8192 | tf_op jit(solution)/shard_map/all_to_all | solution.py:68
  26.4 14.1 %copy-start.6 = (s32[1,8]{1,0:T(1,128)S(1)}, s32[1,8]{1,0:T(1,128)}, u32[]{:S(2)}) copy-start(s32[1,8]{1,0:T(1,128)} %param.21) | copy-start | bytes 100
  26.4 18.3 %copy-start.1 = (bf16[1,8,8,128,128]{4,3,2,1,0:T(8,128)(2,1)S(1)}, bf16[1,8,8,128,128]{4,3,2,1,0:T(8,128)(2,1)}, u32[]{:S(2)}) copy-start(bf16[1,8,8,128,128]{4,3,2,1,0:T(8,128)(2,1)} %param.19) | copy-start | bytes 6291460
  27.4 13.1 %all-to-all-start = ((bf16[16,8,1024]{2,0,1:T(8,128)(2,1)}), bf16[16,8,1024]{2,0,1:T(8,128)(2,1)S(1)}, u32[]{:S(2)}, u32[]{:S(2)}) async-start(bf16[16,8,1024]{2,0,1:T(8,128)(2,1)} %copy.39), calls=%async_computation | async-start | bytes 524288 | tf_op jit(solution)/shard_map/all_to_all | solution.py:52
  36.8 11.8 %copy-start.5 = (s32[1,8,8]{2,1,0:T(8,128)S(1)}, s32[1,8,8]{2,1,0:T(8,128)}, u32[]{:S(2)}) copy-start(s32[1,8,8]{2,1,0:T(8,128)} %param.20) | copy-start | bytes 772
  40.5 22.6 %all-to-all-start.1 = ((bf16[16,8,1024]{2,0,1:T(8,128)(2,1)}), bf16[16,8,1024]{2,0,1:T(8,128)(2,1)}, u32[]{:S(2)}, u32[]{:S(2)}) async-start(bf16[16,8,1024]{2,0,1:T(8,128)(2,1)} %copy.43), calls=%async_computation.1 | async-start | bytes 524288 | tf_op jit(solution)/shard_map/all_to_all | solution.py:53
  63.2 4.8 %copy-start.7 = (bf16[256]{0:T(256)(128)(2,1)S(1)}, bf16[256]{0:T(256)(128)(2,1)}, u32[]{:S(2)}) copy-start(bf16[256]{0:T(256)(128)(2,1)} %param.18) | copy-start | bytes 1540
  63.2 4.8 %copy-start.4 = (bf16[2,16,256]{2,1,0:T(8,128)(2,1)S(1)}, bf16[2,16,256]{2,1,0:T(8,128)(2,1)}, u32[]{:S(2)}) copy-start(bf16[2,16,256]{2,1,0:T(8,128)(2,1)} %param.17) | copy-start | bytes 49156
  63.2 62.9 %all-to-all-start.4 = ((bf16[8,8,128,256]{3,2,1,0:T(8,128)(2,1)}), bf16[8,8,128,256]{3,2,1,0:T(8,128)(2,1)}, u32[]{:S(2)}, u32[]{:S(2)}) async-start(bf16[8,8,128,256]{3,2,1,0:T(8,128)(2,1)} %bitcast.122), calls=%async_computation.4 | async-start | bytes 8388608 | tf_op jit(solution)/shard_map/all_to_all | solution.py:101
  126.0 6.2 %copy-start.2 = (bf16[2,256,256]{2,1,0:T(8,128)(2,1)S(1)}, bf16[2,256,256]{2,1,0:T(8,128)(2,1)}, u32[]{:S(2)}) copy-start(bf16[2,256,256]{2,1,0:T(8,128)(2,1)} %param.22) | copy-start | bytes 786436
  126.0 54.9 %all-to-all-start.3 = ((bf16[8,8,128,256]{3,2,1,0:T(8,128)(2,1)}), bf16[8,8,128,256]{3,2,1,0:T(8,128)(2,1)}, u32[]{:S(2)}, u32[]{:S(2)}) async-start(bf16[8,8,128,256]{3,2,1,0:T(8,128)(2,1)} %bitcast.125), calls=%async_computation.3 | async-start | bytes 8388608 | tf_op jit(solution)/shard_map/all_to_all | solution.py:70
  130.7 60.0 %reduce-scatter.2.cloned.1.call-start = ((), (), s32[]{:S(2)}) async-start(), calls=%async_computation.6 | async-start | bytes 294912 | tf_op jit(solution)/shard_map/reduce_scatter | solution.py:119
  137.3 1.9 copy-start.3
Sparse Core Ops, SparseCore 0:
  143.5 36.9 reduce-scatter.1
where the time goes:
time: 219 us; the launch traced here: 218 us
  blocking collectives  72.9 us (33%)
  local copies, waits for them, and re-layouts  42.6 us (19%)
  waiting for transfers between devices  37.5 us (17%)
  matrix products  23.6 us (11%)
  starting transfers between devices  23.2 us (11%)
  between operations  14.2 us (6%)
  other arithmetic  3.9 us (2%)
    all_gather x1, blocking collectives, body(): full_weight = lax.all_gather(w_one, 'feat', axis=1, tiled=True)  52.5 us
    all_to_all x1, waiting for transfers between devices, body(): lax.all_to_all(picked, 'feat', split_axis=0, concat_axis=0, tiled=True)  37.5 us
    psum x1, blocking collectives, body(): grad_sum = lax.psum(shares, 'grp')  20.5 us
    scatter x1, local copies, waits for them, and re-layouts, body(): outgoing = jnp.zeros((feat_count * capacity, tile_size, hidden_width), jn...  12 us
    dot_general x1, matrix products, body(): jnp.einsum('ftkj,tkij->fti', windows, adj_one[0], preferred_element_type=...  6.42 us
    unnamed x18, local copies, waits for them, and re-layouts  5.78 us
    all_to_all x1, starting transfers between devices, body(): lax.all_to_all(request, 'feat', split_axis=0, concat_axis=0, tiled=True)  5.17 us
    gather x1, local copies, waits for them, and re-layouts, body(): fetched.reshape(feat_count * capacity, tile_size, hidden_width)[target]  4.97 us
  transfers between devices with their start and end apart: 6, of which 1 were waited for; matrix products, arithmetic and copies ran while one was open for 30% of the time, Pallas kernels for 0%

commit v1 on v0

v1 whole, which is shorter than its diff:
```python
import functools

import jax
import jax.numpy as jnp
from jax import lax
from jax.experimental import pallas as pl
from jax.experimental.pallas import tpu as pltpu
from jax.sharding import PartitionSpec as P

BATCH = 4
HEAD = 8
NT = (((1,), (1,)), ((), ()))
TN = (((0,), (0,)), ((), ()))
VMEM = pl.BlockSpec(memory_space=pltpu.VMEM)
SMEM = pl.BlockSpec(memory_space=pltpu.SMEM)
HBM = pl.BlockSpec(memory_space=pltpu.HBM)


def dot(a, b, dims=(((1,), (0,)), ((), ()))):
    return lax.dot_general(a, b, dims, preferred_element_type=jnp.float32)


def exchange(array, axis, mask):
    size = lax.axis_size(axis)
    return lax.ppermute(array, axis, [(i, i ^ mask) for i in range(size)])


class Plan:
    def __init__(self, group_tiles, fan_one, own, fan_two, zero_tile):
        self.group_tiles, self.fan_one, self.own, self.fan_two = group_tiles, fan_one, own, fan_two
        self.entries = own * fan_two
        self.dense = self.entries == group_tiles
        self.slots = group_tiles if self.dense else self.entries + own
        self.steps = -(-self.slots // BATCH)
        self.padded = self.steps * BATCH
        self.place = 1
        self.cols_two = self.place + group_tiles
        self.count_two = self.cols_two + self.entries
        self.cols_one = self.count_two + own
        self.count_one = self.cols_one + group_tiles * fan_one
        self.tile_at = HEAD
        self.slot_at = self.tile_at + self.padded + BATCH
        self.column_at = self.slot_at + self.padded + BATCH
        self.entry_at = self.column_at + (self.padded + BATCH) * fan_one
        self.table = self.entry_at + self.entries
        self.zero_tile = zero_tile


def prepare_kernel(
    plan, ints, bias_ref, adj_one_ref, adj_two_ref, w_ref, cot_ref,
    d_ref, adj_one, adj_two, w_two, bias, table,
    cot, back, inverse, active, sems, adj_sems,
):
    own, fan, fan_one = plan.own, plan.fan_two, plan.fan_one
    tile = adj_two.shape[-1]
    hidden = w_two.shape[-1]
    first = ints[0] * own
    own_slot = first if plan.dense else plan.entries

    copies = [
        pltpu.make_async_copy(source, to, sems.at[i])
        for i, (source, to) in enumerate(((w_ref, w_two), (cot_ref, cot), (adj_two_ref, adj_two)))
    ]
    for copy in copies:
        copy.start()

    def adj_copy(i):
        t = table[plan.tile_at + i]
        return pltpu.make_async_copy(adj_one_ref.at[t], adj_one.at[i], adj_sems.at[i])

    @pl.loop(0, plan.group_tiles, unroll=8)
    def _(t):
        inverse[ints[plan.place + t]] = t

    @pl.loop(0, own)
    def _(p):
        count = ints[plan.count_two + p]
        for k in range(fan):
            e = p * fan + k
            slot = ints[plan.cols_two + e] if plan.dense else e
            live = k < count
            table[plan.entry_at + e] = jnp.where(live, slot, own_slot)
            if plan.dense:
                mine = jnp.logical_and(slot >= own_slot, slot < own_slot + own)
                live = jnp.logical_or(live, mine)
            active[slot] = live.astype(jnp.int32)
        if not plan.dense:
            active[plan.entries + p] = 1

    def visit(s, n):
        if plan.dense:
            placed = s
        else:
            named = ints[plan.cols_two + jnp.minimum(s, plan.entries - 1)]
            placed = jnp.where(s < plan.entries, named, first + s - plan.entries)
        table[plan.tile_at + n] = inverse[placed]
        table[plan.slot_at + n] = s
        return n + active[s]

    n = lax.fori_loop(0, plan.slots, visit, jnp.int32(0), unroll=8)
    steps = lax.div(n + BATCH - 1, BATCH)
    table[0] = steps
    table[1] = own_slot

    @pl.loop(n, plan.padded + BATCH)
    def _(i):
        table[plan.tile_at + i] = 0
        table[plan.slot_at + i] = plan.slots + lax.rem(i, BATCH)

    @pl.loop(0, steps + 1)
    def _(step):
        for b in range(BATCH):
            i = step * BATCH + b
            t = table[plan.tile_at + i]
            count = ints[plan.count_one + t]
            for k in range(fan_one):
                column = ints[plan.cols_one + t * fan_one + k]
                table[plan.column_at + i * fan_one + k] = jnp.where(k < count, column, plan.zero_tile)

    @pl.loop(0, steps)
    def _(step):
        for b in range(BATCH):
            adj_copy(step * BATCH + b).start()

    for b in range(BATCH):
        d_ref[plan.slots + b] = jnp.zeros((hidden, tile), d_ref.dtype)
    if not plan.dense:
        for p in range(own):
            d_ref[plan.entries + p] = jnp.zeros((hidden, tile), d_ref.dtype)
    bias[...] = jnp.broadcast_to(bias_ref[...], (tile, hidden)).T

    copies[0].wait()
    copies[1].wait()
    back[...] = dot(w_two[1], cot[...], NT).astype(back.dtype)
    copies[2].wait()

    @pl.loop(0, own)
    def _(p):
        @pl.loop(ints[plan.count_two + p], fan)
        def _(k):
            adj_two[p, k] = jnp.zeros((tile, tile), adj_two.dtype)

    for p in range(own):
        tiles = jnp.concatenate([adj_two[p, k] for k in range(fan)], axis=1)
        term = dot(back[:, p * tile : (p + 1) * tile], tiles).astype(d_ref.dtype)
        for k in range(fan):
            e = p * fan + k
            slot = ints[plan.cols_two + e] if plan.dense else e
            d_ref[slot] = term[:, k * tile : (k + 1) * tile]

    self_rows = dot(w_two[0], cot[...], NT)
    for p in range(own):
        mine = self_rows[:, p * tile : (p + 1) * tile] + d_ref[own_slot + p].astype(jnp.float32)
        d_ref[own_slot + p] = mine.astype(d_ref.dtype)

    @pl.loop(0, steps)
    def _(step):
        for b in range(BATCH):
            adj_copy(step * BATCH + b).wait()


def layer_one_kernel(plan, blocks, table, *refs):
    x_refs = refs[:blocks]
    bias, adj_one, d_ref, even_ref, odd_ref, h_ref, weight, total, both, downs = refs[blocks:]
    fan = plan.fan_one
    tile = adj_one.shape[-1]
    hidden = bias.shape[0]
    features = x_refs[0].shape[0] * blocks
    steps = table[0]

    def x_tile(t):
        at = pl.ds(pl.multiple_of(t * tile, tile), tile)
        return jnp.concatenate([x[:, at] for x in x_refs], axis=0)

    def lanes(b):
        return slice(b * tile, (b + 1) * tile)

    def aggregate(step):
        at = lax.rem(step, 2)
        for b in range(BATCH):
            i = step * BATCH + b
            j = jnp.minimum(i, plan.padded - 1)
            x_all = [x_tile(table[plan.column_at + i * fan + k]) for k in range(fan)]
            tiles = [adj_one[j, k] for k in range(fan)]
            agg = dot(jnp.concatenate(x_all, axis=1), jnp.concatenate(tiles, axis=1), NT)
            both[at, :features, lanes(b)] = x_tile(table[plan.tile_at + i])
            both[at, features:, lanes(b)] = agg.astype(both.dtype)

    def activate(step):
        at = lax.rem(step, 2)
        for b in range(0, BATCH, 2):
            z = dot(weight[...], both[at, :, b * tile : (b + 2) * tile])
            for c in range(2):
                v = z[:, lanes(c)] + bias[...]
                s = 0.5 * jnp.tanh(0.5 * v) + 0.5
                h = v * s
                slope = s + h * (1.0 - s)
                slot = table[plan.slot_at + step * BATCH + b + c]
                h_ref[slot] = h.astype(h_ref.dtype)
                down = d_ref[slot].astype(jnp.float32) * slope
                downs[at, :, lanes(b + c)] = down.astype(downs.dtype)

    def contract(step):
        at = lax.rem(step + 2, 2)
        total[...] += dot(both[at], downs[at], NT)

    for part in range(2):
        at = pl.ds(plan.group_tiles * tile + part * hidden, hidden)
        w = jnp.concatenate([x[:, at] for x in x_refs], axis=0)
        weight[:, part * features : (part + 1) * features] = w.astype(jnp.float32).T.astype(weight.dtype)
    total[...] = jnp.zeros_like(total)
    both[1] = jnp.zeros(both.shape[1:], both.dtype)
    downs[1] = jnp.zeros(downs.shape[1:], downs.dtype)
    aggregate(0)

    @pl.loop(0, steps)
    def _(step):
        contract(step - 1)
        activate(step)
        aggregate(step + 1)

    contract(steps - 1)
    half = even_ref.shape[0]
    share = features // (2 * half)
    for m in range(2 * half):
        out = even_ref if m % 2 == 0 else odd_ref
        for part in range(2):
            at = part * features + m * share
            out[m // 2, part] = total[at : at + share]


def layer_two_kernel(plan, table, h_ref, adj_two, w_ref, out_ref, agg, out, sems):
    own, fan = plan.own, plan.fan_two
    tile = adj_two.shape[-1]
    own_slot = table[1]
    for p in range(own):
        h_all = [h_ref[table[plan.entry_at + p * fan + k]] for k in range(fan)]
        tiles = [adj_two[p, k] for k in range(fan)]
        rows = dot(jnp.concatenate(h_all, axis=1), jnp.concatenate(tiles, axis=1), NT)
        agg[p] = rows.astype(agg.dtype)
    copies = []
    for p in range(own):
        rows = dot(h_ref[own_slot + p], w_ref[0], TN) + dot(agg[p], w_ref[1], TN)
        out[p] = rows.astype(out.dtype)
        copies.append(pltpu.make_async_copy(out.at[p], out_ref.at[p], sems.at[p]))
        copies[-1].start()
    for copy in copies:
        copy.wait()


def call_prepare(plan, ints, bias, adj_one, adj_two, w_two, cot):
    own, fan, tile, _ = adj_two.shape
    hidden = w_two.shape[-1]
    kind = adj_one.dtype
    return pl.pallas_call(
        functools.partial(prepare_kernel, plan),
        out_shape=(
            jax.ShapeDtypeStruct((plan.slots + BATCH, hidden, tile), kind),
            jax.ShapeDtypeStruct((plan.padded, plan.fan_one, tile, tile), kind),
            jax.ShapeDtypeStruct(adj_two.shape, kind),
            jax.ShapeDtypeStruct(w_two.shape, kind),
            jax.ShapeDtypeStruct((hidden, tile), jnp.float32),
            jax.ShapeDtypeStruct((plan.table,), jnp.int32),
        ),
        in_specs=[SMEM, VMEM] + [HBM] * 4,
        out_specs=(VMEM,) * 5 + (SMEM,),
        scratch_shapes=[
            pltpu.VMEM((own * tile, hidden), kind),
            pltpu.VMEM((hidden, own * tile), kind),
            pltpu.SMEM((plan.group_tiles,), jnp.int32),
            pltpu.SMEM((plan.slots,), jnp.int32),
            pltpu.SemaphoreType.DMA((3,)),
            pltpu.SemaphoreType.DMA((plan.padded,)),
        ],
        compiler_params=pltpu.CompilerParams(vmem_limit_bytes=34 << 20),
        cost_estimate=pl.CostEstimate(
            flops=2 * plan.entries * tile * tile * hidden, bytes_accessed=20 << 20, transcendentals=0
        ),
        name="prepare",
    )(ints, bias, adj_one, adj_two, w_two, cot)


def call_layer_one(plan, feat_count, table, gathered, bias, adj_one, down):
    blocks = len(gathered)
    tile = adj_one.shape[-1]
    hidden = bias.shape[0]
    features = gathered[0].shape[0] * blocks
    kind = adj_one.dtype
    share = jax.ShapeDtypeStruct((feat_count // 2, 2, features // feat_count, hidden), jnp.float32)
    return pl.pallas_call(
        functools.partial(layer_one_kernel, plan, blocks),
        out_shape=(share, share, jax.ShapeDtypeStruct(down.shape, kind)),
        in_specs=[SMEM] + [VMEM] * (blocks + 3),
        out_specs=(VMEM,) * 3,
        scratch_shapes=[
            pltpu.VMEM((hidden, 2 * features), kind),
            pltpu.VMEM((2 * features, hidden), jnp.float32),
            pltpu.VMEM((2, 2 * features, BATCH * tile), kind),
            pltpu.VMEM((2, hidden, BATCH * tile), kind),
        ],
        compiler_params=pltpu.CompilerParams(vmem_limit_bytes=12 << 20),
        cost_estimate=pl.CostEstimate(
            flops=2 * plan.slots * tile * 2 * features * hidden * 3,
            bytes_accessed=20 << 20,
            transcendentals=plan.slots * tile * hidden,
        ),
        name="layer_one",
    )(table, *gathered, bias, adj_one, down)


def call_layer_two(plan, table, h_tiles, adj_two, w_two):
    own, fan, tile, _ = adj_two.shape
    hidden = w_two.shape[-1]
    kind = h_tiles.dtype
    return pl.pallas_call(
        functools.partial(layer_two_kernel, plan),
        out_shape=jax.ShapeDtypeStruct((own, tile, hidden), kind),
        in_specs=[SMEM, VMEM, VMEM, VMEM],
        out_specs=HBM,
        scratch_shapes=[
            pltpu.VMEM((own, hidden, tile), kind),
            pltpu.VMEM((own, tile, hidden), kind),
            pltpu.SemaphoreType.DMA((own,)),
        ],
        compiler_params=pltpu.CompilerParams(vmem_limit_bytes=12 << 20),
        cost_estimate=pl.CostEstimate(
            flops=2 * plan.entries * tile * tile * hidden, bytes_accessed=8 << 20, transcendentals=0
        ),
        name="layer_two",
    )(table, h_tiles, adj_two, w_two)


def body(
    x_feat,
    place,
    adj_one,
    cols_one,
    count_one,
    w_one,
    bias_one,
    adj_two,
    cols_two,
    count_two,
    w_two,
    cotangent,
):
    x_local = x_feat[0]
    feat_dev = x_local.shape[0]
    tile = adj_one.shape[-1]
    own, fan_two = adj_two.shape[1:3]
    hidden = w_two.shape[-1]
    feat_count = lax.axis_size("feat")
    plan = Plan(place.shape[1], adj_one.shape[2], own, fan_two, place.shape[1] + 2 * hidden // tile)

    nothing = jnp.zeros((feat_dev, tile), x_local.dtype)
    packed = jnp.concatenate([x_local, w_one[0], w_one[1], nothing], axis=1)
    near = [packed] + [exchange(packed, "feat", m) for m in range(2, feat_count, 2)]
    far = [exchange(packed, "feat", 1)]

    me = lax.axis_index("feat").astype(jnp.int32).reshape(1)
    ints = jnp.concatenate(
        [me]
        + [a.reshape(-1) for a in (place, cols_two, count_two, cols_one, count_one)]
    )
    down, adj_near, adj_far, weights, bias, table = call_prepare(
        plan, ints, bias_one.astype(jnp.float32).reshape(1, hidden), adj_one[0], adj_two[0], w_two, cotangent[0]
    )
    near[1:], down = lax.optimization_barrier((near[1:], down))
    far += [exchange(block, "feat", 1) for block in near[1:]]
    gathered = [block for pair in zip(near, far) for block in pair]
    merge = max(1, 16 // feat_dev)
    if merge > 1:
        gathered = [
            jnp.concatenate(gathered[i : i + merge], axis=0) for i in range(0, feat_count, merge)
        ]
    even, odd, h_tiles = call_layer_one(plan, feat_count, table, gathered, bias, adj_near, down)
    layer_out = call_layer_two(plan, table, h_tiles, adj_far, weights)

    even = even + exchange(odd, "feat", 1)
    grad = even[0]
    for received in [exchange(even[j], "feat", 2 * j) for j in range(1, feat_count // 2)]:
        grad = grad + received
    level = [grad] + [exchange(grad, "grp", m) for m in range(1, lax.axis_size("grp"))]
    while len(level) > 1:
        level = [level[i] + level[i + 1] for i in range(0, len(level), 2)]
    return (layer_out.reshape(1, own * tile, hidden), level[0])


def solution(mesh):
    in_specs = (
        P("grp", "feat", None),
        P("grp", None),
        P("grp", None, None, None, None),
        P("grp", None, None),
        P("grp", None),
        P(None, "feat", None),
        P(),
        P("grp", "feat", None, None, None),
        P("grp", "feat", None),
        P("grp", "feat"),
        P(),
        P("grp", "feat", None),
    )
    out_specs = (P("grp", "feat", None), P(None, "feat", None))
    return jax.shard_map(body, mesh=mesh, in_specs=in_specs, out_specs=out_specs, check_vma=False)
```

time: 219 us -> 47.9 us (0.22)
  blocking collectives: 72.9 us -> 0 us
  local copies, waits for them, and re-layouts: 42.6 us -> 6.73 us
  waiting for transfers between devices: 37.5 us -> 8.01 us
  matrix products: 23.6 us -> 0 us
  Pallas kernels: 0 us -> 15.6 us
  between operations: 14.2 us -> 0.73 us
  starting transfers between devices: 23.2 us -> 14.2 us
    all_gather x1 -> x0, blocking collectives: 52.5 us -> none  [body(): full_weight = lax.all_gather(w_one, 'feat', axis=1, tiled=True)]
    all_to_all x5 -> x0, waiting for transfers between devices: 37.5 us -> none  [the longest x1 37.5 us: body(): lax.all_to_all(picked, 'feat', split_axis=0, concat_axis=0, tiled=True)]
    dot_general x12 -> x0, matrix products: 23.6 us -> none  [the longest x1 6.42 us: body(): jnp.einsum('ftkj,tkij->fti', windows, adj_one[0], preferred_element_type=...]
    all_to_all x5 -> x0, starting transfers between devices: 23 us -> none  [the longest x1 5.17 us: body(): lax.all_to_all(request, 'feat', split_axis=0, concat_axis=0, tiled=True)]
    psum x1 -> x0, blocking collectives: 20.5 us -> none  [body(): grad_sum = lax.psum(shares, 'grp')]
    pallas_call x0 -> x3, Pallas kernels: none -> 15.6 us  [the longest x1 6.56 us: call_layer_one(): pl.pallas_call(functools.partial(layer_one_kernel, plan, blocks), out_sha...]
    ppermute x0 -> x14, starting transfers between devices: none -> 14.2 us  [exchange(): return lax.ppermute(array, axis, [(i, i ^ mask) for i in range(size)])]
    gather x7 -> x0, local copies, waits for them, and re-layouts: 13.3 us -> none  [the longest x1 4.97 us: body(): fetched.reshape(feat_count * capacity, tile_size, hidden_width)[target]]
  transfers between devices with their start and end apart: 6 -> 14, of which waited for: 1 -> 7; matrix products, arithmetic and copies ran while one was open for 30% -> 6% of each run, Pallas kernels for 0% -> 19%
where the time goes in v1:
time: 47.9 us; the launch traced here: 47.5 us
  Pallas kernels  15.6 us (33%)
  starting transfers between devices  14.2 us (30%)
  waiting for transfers between devices  8.01 us (17%)
  local copies, waits for them, and re-layouts  6.73 us (14%)
  other arithmetic  2.33 us (5%)
  between operations  0.73 us (2%)
    ppermute x14, starting transfers between devices, exchange(): return lax.ppermute(array, axis, [(i, i ^ mask) for i in range(size)])  14.2 us
    ppermute x14, waiting for transfers between devices, exchange(): return lax.ppermute(array, axis, [(i, i ^ mask) for i in range(size)])  8.01 us
    pallas_call x1, Pallas kernels, call_layer_one(): pl.pallas_call(functools.partial(layer_one_kernel, plan, blocks), out_sha...  6.56 us
    pallas_call x1, Pallas kernels, call_prepare(): pl.pallas_call(functools.partial(prepare_kernel, plan), out_shape=(jax.Sh...  6.07 us
    unnamed x7, local copies, waits for them, and re-layouts  4.35 us
    pallas_call x1, Pallas kernels, call_layer_two(): pl.pallas_call(functools.partial(layer_two_kernel, plan), out_shape=jax.S...  2.93 us
    concatenate x1, other arithmetic, body(): packed = jnp.concatenate([x_local, w_one[0], w_one[1], nothing], axis=1)  1.01 us
  transfers between devices with their start and end apart: 14, of which 7 were waited for; matrix products, arithmetic and copies ran while one was open for 6% of the time, Pallas kernels for 19%

profile of v1, /device:TPU:0, one launch (start us, length us, event | category | flops | bytes accessed | tf_op | source)
XLA Modules:
  0.0 47.5 jit_solution(3547909121491395680)
XLA Ops:
  0.6 0.7 %slice_bitcast_fusion.5 = (bf16[16,256]{1,0:T(8,128)(2,1)S(1)}, bf16[16,256]{1,0:T(8,128)(2,1)S(1)}) fusion(bf16[2,16,256]{2,1,0:T(8,128)(2,1)} %param.17), kind=kLoop, calls=%fused_computation.10 | loop fusion | bytes 32768 | tf_op jit(solution)/shard_map/squeeze | solution.py:356
  1.4 1.0 %maximum_maximum_fusion.refs_0_ = bf16[16,8832]{1,0:T(8,128)(2,1)S(1)} fusion(bf16[16,256]{1,0:T(8,128)(2,1)S(1)} %get-tuple-element.32, bf16[16,256]{1,0:T(8,128)(2,1)S(1)} %get-tuple-element.31, bf16[16,8192]{1,0:T(8,128)(2,1)} %bitcast.33, bf16[8832]{0:T(1024)(128)(2,1)S(1)} %pad.3.clone), kind=kLoop, calls=%fused_computation | loop fusion | flops 1130496 | bytes 578816 | tf_op jit(solution)/shard_map/concatenate | solution.py:356
  2.4 4.0 %collective-permute-start.3 = (bf16[16,8832]{1,0:T(8,128)(2,1)S(1)}, bf16[16,8832]{1,0:T(8,128)(2,1)S(1)}, u32[]{:S(2)}, u32[]{:S(2)}) collective-permute-start(bf16[16,8832]{1,0:T(8,128)(2,1)S(1)} %maximum_maximum_fusion.refs_0_), channel_id=1, source_target_pairs={{0,24},{4,28},{8,16},{12,20},{16,8},{20,12},{24,0},{28,4},{1,25},{... | collective-permute-start | bytes 847880 | tf_op jit(solution)/shard_map/ppermute | solution.py:25
  6.3 0.5 %collective-permute-start.2 = (bf16[16,8832]{1,0:T(8,128)(2,1)S(1)}, bf16[16,8832]{1,0:T(8,128)(2,1)S(1)}, u32[]{:S(2)}, u32[]{:S(2)}) collective-permute-start(bf16[16,8832]{1,0:T(8,128)(2,1)S(1)} %maximum_maximum_fusion.refs_0_), channel_id=1, source_target_pairs={{0,16},{4,20},{8,24},{12,28},{16,0},{20,4},{24,8},{28,12},{1,17},{... | collective-permute-start | bytes 847880 | tf_op jit(solution)/shard_map/ppermute | solution.py:25
  6.8 0.1 collective-permute-start.1
  7.0 0.0 collective-permute-start
  7.0 0.8 %reshape.32 = s32[64]{0:T(128)S(1)} reshape(s32[1,8,8]{2,1,0:T(8,128)} %param.20) | data formatting | bytes 512 | tf_op jit(solution)/shard_map/reshape | solution.py:363
  7.7 0.7 %reshape.39 = f32[256]{0:T(256)S(1)} convert(bf16[256]{0:T(256)(128)(2,1)} %param.18) | non-fusion elementwise | flops 256 | bytes 1536 | tf_op jit(solution)/shard_map/reshape | solution.py:366
  8.4 0.8 %copy.14 = s32[1,64,4]{2,1,0:T(8,128)S(1)} copy(s32[1,64,4]{1,2,0:T(4,128)} %param.15) | data formatting | bytes 2048 | tf_op args[3]
  9.2 0.1 reshape.34
  9.3 0.8 %concatenate.6.ints = s32[457]{0:T(512)S(1)} concatenate(s32[1]{0:T(128)} %bitcast, s32[64]{0:T(128)} %bitcast.34, s32[64]{0:T(128)S(1)} %reshape.32, s32[8]{0:T(128)} %bitcast.35, s32[256]{0:T(256)S(1)} %reshape.34, s32[64]{0:T(128)} %bitcast.36), dimensions={0} | concatenate | bytes 3656 | tf_op jit(solution)/shard_map/concatenate | solution.py:361
  10.1 0.0 copy-start
  10.1 1.6 %copy-done = bf16[1,8,8,128,128]{4,3,2,1,0:T(8,128)(2,1)S(1)} copy-done((bf16[1,8,8,128,128]{4,3,2,1,0:T(8,128)(2,1)S(1)}, bf16[1,8,8,128,128]{4,3,2,1,0:T(8,128)(2,1)}, u32[]{:S(2)}) %copy-start) | copy-done | bytes 2097176
  11.6 0.0 copy-start.1
  11.6 1.0 %copy-done.1 = bf16[1,1024,256]{2,1,0:T(8,128)(2,1)S(1)} copy-done((bf16[1,1024,256]{2,1,0:T(8,128)(2,1)S(1)}, bf16[1,1024,256]{2,1,0:T(8,128)(2,1)}, u32[]{:S(2)}) %copy-start.1) | copy-done | bytes 524312
  12.7 0.0 copy-start.2
  12.7 0.9 %copy-done.2 = bf16[2,256,256]{2,1,0:T(8,128)(2,1)S(1)} copy-done((bf16[2,256,256]{2,1,0:T(8,128)(2,1)S(1)}, bf16[2,256,256]{2,1,0:T(8,128)(2,1)}, u32[]{:S(2)}) %copy-start.2) | copy-done | bytes 262168
  13.6 6.1 %prepare.1 = (bf16[68,256,128]{2,1,0:T(8,128)(2,1)S(1)}, bf16[64,4,128,128]{3,2,1,0:T(8,128)(2,1)S(1)}, bf16[8,8,128,128]{3,2,1,0:T(8,128)(2,1)S(1)}, bf16[2,256...) custom-call(s32[457]{0:T(512)S(1)} %concatenate.6.ints, f32[1,256]{1,0:T(1,128)S(1)} %bitcast.30, ...), custom_call_target="tpu_custom_call" | custom-call | flops 536870912 | bytes 20971520 | tf_op jit(solution)/shard_map/prepare/pallas_call | solution.py:255
  19.7 0.0 collective-permute-done.3.refs_6_
  19.7 0.0 collective-permute-done.2.refs_4_
  19.7 0.0 collective-permute-done.1.refs_2_
  19.7 0.4 collective-permute-start.4
  20.1 0.2 collective-permute-start.5
  20.3 0.3 collective-permute-start.6
  20.7 0.0 collective-permute-done.refs_1_
  20.7 0.7 %collective-permute-done.4.refs_3_ = bf16[16,8832]{1,0:T(8,128)(2,1)S(1)} collective-permute-done((bf16[16,8832]{1,0:T(8,128)(2,1)S(1)}, bf16[16,8832]{1,0:T(8,128)(2,1)S(1)}, u32[]{:S(2)}, u32[]{:S(2)}) %collective-permute-start.4) | collective-permute-done | bytes 282656 | tf_op jit(solution)/shard_map/ppermute | solution.py:25
  21.4 0.4 collective-permute-done.5.refs_5_
  21.8 0.4 collective-permute-done.6.refs_7_
  22.2 6.6 %layer_one.1 = (f32[4,2,16,256]{3,2,1,0:T(8,128)S(1)}, f32[4,2,16,256]{3,2,1,0:T(8,128)S(1)}, bf16[68,256,128]{2,1,0:T(8,128)(2,1)S(1)}) custom-call(s32[480]{0:T(512)S(1)} %get-tuple-element.15.table, bf16[16,8832]{1,0:T(8,128)(2,1)S(1)} %maximum_maximum_fusion.refs_0_, bf16[16,8832]{1,0:T(8,128)(2,1)S(1)} %collective-permute-done.refs_1_, ...), custom_call_target="tpu_custom_call" | custom-call | flops 3221225472 | bytes 20971520 | tf_op jit(solution)/shard_map/layer_one/pallas_call | solution.py:290
  28.8 0.1 collective-permute-start.7
  28.8 1.3 %collective-permute-done.7 = f32[4,2,16,256]{3,2,1,0:T(8,128)S(1)} collective-permute-done((f32[4,2,16,256]{3,2,1,0:T(8,128)S(1)}, f32[4,2,16,256]{3,2,1,0:T(8,128)S(1)}, u32[]{:S(2)}, u32[]{:S(2)}) %collective-permute-start.7) | collective-permute-done | bytes 131104 | tf_op jit(solution)/shard_map/ppermute | solution.py:25
  30.2 0.8 %collective-permute-start.8 = (f32[2,16,256]{2,1,0:T(8,128)S(1)}, f32[2,16,256]{2,1,0:T(8,128)S(1)}, u32[]{:S(2)}, u32[]{:S(2)}) collective-permute-start(f32[2,16,256]{2,1,0:T(8,128)S(1)} %get-tuple-element.28), channel_id=1, source_target_pairs={{0,8},{4,12},{8,0},{12,4},{16,24},{20,28},{24,16},{28,20},{1,9},{5... | collective-permute-start | bytes 98312 | tf_op jit(solution)/shard_map/ppermute | solution.py:25
  31.1 3.3 %collective-permute-start.10 = (f32[2,16,256]{2,1,0:T(8,128)S(1)}, f32[2,16,256]{2,1,0:T(8,128)S(1)}, u32[]{:S(2)}, u32[]{:S(2)}) collective-permute-start(f32[2,16,256]{2,1,0:T(8,128)S(1)} %get-tuple-element.29), channel_id=1, source_target_pairs={{0,24},{4,28},{8,16},{12,20},{16,8},{20,12},{24,0},{28,4},{1,25},{... | collective-permute-start | bytes 98312 | tf_op jit(solution)/shard_map/ppermute | solution.py:25
  34.3 0.0 collective-permute-start.9
  34.3 0.0 collective-permute-done.8
  34.3 2.2 %collective-permute-done.10 = f32[2,16,256]{2,1,0:T(8,128)S(1)} collective-permute-done((f32[2,16,256]{2,1,0:T(8,128)S(1)}, f32[2,16,256]{2,1,0:T(8,128)S(1)}, u32[]{:S(2)}, u32[]{:S(2)}) %collective-permute-start.10) | collective-permute-done | bytes 32800 | tf_op jit(solution)/shard_map/ppermute | solution.py:25
  36.6 1.7 %collective-permute-done.9 = f32[2,16,256]{2,1,0:T(8,128)S(1)} collective-permute-done((f32[2,16,256]{2,1,0:T(8,128)S(1)}, f32[2,16,256]{2,1,0:T(8,128)S(1)}, u32[]{:S(2)}, u32[]{:S(2)}) %collective-permute-start.9) | collective-permute-done | bytes 32800 | tf_op jit(solution)/shard_map/ppermute | solution.py:25
  38.3 3.8 %collective-permute-start.13 = (f32[2,16,256]{2,1,0:T(8,128)S(1)}, f32[2,16,256]{2,1,0:T(8,128)S(1)}, u32[]{:S(2)}, u32[]{:S(2)}) collective-permute-start(f32[2,16,256]{2,1,0:T(8,128)S(1)} %fusion.2), channel_id=1, source_target_pairs={{0,3},{1,2},{2,1},{3,0},{4,7},{5,6},{6,5},{7,4},{8,11},{9,10},{10,... | collective-permute-start | bytes 98312 | tf_op jit(solution)/shard_map/ppermute | solution.py:25
  42.1 0.3 collective-permute-start.12
  42.4 0.3 collective-permute-start.11
  42.7 2.9 %layer_two.1 = bf16[8,128,256]{2,1,0:T(8,128)(2,1)} custom-call(s32[480]{0:T(512)S(1)} %get-tuple-element.15.table, bf16[68,256,128]{2,1,0:T(8,128)(2,1)S(1)} %get-tuple-element.23.h_ref, bf16[8,8,128,128]{3,2,1,0:T(8,128)(2,1)S(1)} %get-tuple-element.24.adj_two, bf16[2,256,256]{2,1,0:T(8,128)(2,1)S(1)} %get-tuple-element.25.w_ref), custom_call_target="tpu_custom_call" | custom-call | flops 536870912 | bytes 8388608 | tf_op jit(solution)/shard_map/layer_two/pallas_call | solution.py:315
  45.7 0.0 collective-permute-done.13
  45.7 1.2 %collective-permute-done.12 = f32[2,16,256]{2,1,0:T(8,128)S(1)} collective-permute-done((f32[2,16,256]{2,1,0:T(8,128)S(1)}, f32[2,16,256]{2,1,0:T(8,128)S(1)}, u32[]{:S(2)}, u32[]{:S(2)}) %collective-permute-start.12) | collective-permute-done | bytes 32800 | tf_op jit(solution)/shard_map/ppermute | solution.py:25
  46.9 0.0 collective-permute-done.11
  46.9 0.6 %add_add_fusion = f32[2,16,256]{2,1,0:T(8,128)} fusion(f32[2,16,256]{2,1,0:T(8,128)S(1)} %collective-permute-done.12, f32[2,16,256]{2,1,0:T(8,128)S(1)} %collective-permute-done.13, f32[2,16,256]{2,1,0:T(8,128)S(1)} %fusion.2, f32[2,16,256]{2,1,0:T(8,128)S(1)} %collective-permute-done.11), kind=kLoop, calls=%fused_computation.8 | loop fusion | flops 24576 | bytes 163840 | tf_op jit(solution)/shard_map/add | solution.py:385
  (5 shorter events, 0.1 us)
Async XLA Ops:
  2.4 17.3 %collective-permute-start.3 = (bf16[16,8832]{1,0:T(8,128)(2,1)S(1)}, bf16[16,8832]{1,0:T(8,128)(2,1)S(1)}, u32[]{:S(2)}, u32[]{:S(2)}) collective-permute-start(bf16[16,8832]{1,0:T(8,128)(2,1)S(1)} %maximum_maximum_fusion.refs_0_), channel_id=1, source_target_pairs={{0,24},{4,28},{8,16},{12,20},{16,8},{20,12},{24,0},{28,4},{1,25},{... | collective-permute-start | bytes 847880 | tf_op jit(solution)/shard_map/ppermute | solution.py:25
  6.3 13.4 %collective-permute-start.2 = (bf16[16,8832]{1,0:T(8,128)(2,1)S(1)}, bf16[16,8832]{1,0:T(8,128)(2,1)S(1)}, u32[]{:S(2)}, u32[]{:S(2)}) collective-permute-start(bf16[16,8832]{1,0:T(8,128)(2,1)S(1)} %maximum_maximum_fusion.refs_0_), channel_id=1, source_target_pairs={{0,16},{4,20},{8,24},{12,28},{16,0},{20,4},{24,8},{28,12},{1,17},{... | collective-permute-start | bytes 847880 | tf_op jit(solution)/shard_map/ppermute | solution.py:25
  6.8 12.9 %collective-permute-start.1 = (bf16[16,8832]{1,0:T(8,128)(2,1)S(1)}, bf16[16,8832]{1,0:T(8,128)(2,1)S(1)}, u32[]{:S(2)}, u32[]{:S(2)}) collective-permute-start(bf16[16,8832]{1,0:T(8,128)(2,1)S(1)} %maximum_maximum_fusion.refs_0_), channel_id=1, source_target_pairs={{0,8},{4,12},{8,0},{12,4},{16,24},{20,28},{24,16},{28,20},{1,9},{5... | collective-permute-start | bytes 847880 | tf_op jit(solution)/shard_map/ppermute | solution.py:25
  7.0 13.7 %collective-permute-start = (bf16[16,8832]{1,0:T(8,128)(2,1)S(1)}, bf16[16,8832]{1,0:T(8,128)(2,1)S(1)}, u32[]{:S(2)}, u32[]{:S(2)}) collective-permute-start(bf16[16,8832]{1,0:T(8,128)(2,1)S(1)} %maximum_maximum_fusion.refs_0_), channel_id=1, source_target_pairs={{0,4},{4,0},{8,12},{12,8},{16,20},{20,16},{24,28},{28,24},{1,5},{5... | collective-permute-start | bytes 847880 | tf_op jit(solution)/shard_map/ppermute | solution.py:25
  10.1 1.6 %copy-start = (bf16[1,8,8,128,128]{4,3,2,1,0:T(8,128)(2,1)S(1)}, bf16[1,8,8,128,128]{4,3,2,1,0:T(8,128)(2,1)}, u32[]{:S(2)}) copy-start(bf16[1,8,8,128,128]{4,3,2,1,0:T(8,128)(2,1)} %param.19) | copy-start | bytes 6291460
  11.6 1.0 %copy-start.1 = (bf16[1,1024,256]{2,1,0:T(8,128)(2,1)S(1)}, bf16[1,1024,256]{2,1,0:T(8,128)(2,1)}, u32[]{:S(2)}) copy-start(bf16[1,1024,256]{2,1,0:T(8,128)(2,1)} %param.23) | copy-start | bytes 1572868
  12.7 0.9 %copy-start.2 = (bf16[2,256,256]{2,1,0:T(8,128)(2,1)S(1)}, bf16[2,256,256]{2,1,0:T(8,128)(2,1)}, u32[]{:S(2)}) copy-start(bf16[2,256,256]{2,1,0:T(8,128)(2,1)} %w_ref.1) | copy-start | bytes 786436
  19.7 1.6 %collective-permute-start.4 = (bf16[16,8832]{1,0:T(8,128)(2,1)S(1)}, bf16[16,8832]{1,0:T(8,128)(2,1)S(1)}, u32[]{:S(2)}, u32[]{:S(2)}) collective-permute-start(bf16[16,8832]{1,0:T(8,128)(2,1)S(1)} %collective-permute-done.1.refs_2_), channel_id=1, source_target_pairs={{0,4},{4,0},{8,12},{12,8},{16,20},{20,16},{24,28},{28,24},{1,5},{5... | collective-permute-start | bytes 847880 | tf_op jit(solution)/shard_map/ppermute | solution.py:25
  20.1 1.6 %collective-permute-start.5 = (bf16[16,8832]{1,0:T(8,128)(2,1)S(1)}, bf16[16,8832]{1,0:T(8,128)(2,1)S(1)}, u32[]{:S(2)}, u32[]{:S(2)}) collective-permute-start(bf16[16,8832]{1,0:T(8,128)(2,1)S(1)} %collective-permute-done.2.refs_4_), channel_id=1, source_target_pairs={{0,4},{4,0},{8,12},{12,8},{16,20},{20,16},{24,28},{28,24},{1,5},{5... | collective-permute-start | bytes 847880 | tf_op jit(solution)/shard_map/ppermute | solution.py:25
  20.3 1.9 %collective-permute-start.6 = (bf16[16,8832]{1,0:T(8,128)(2,1)S(1)}, bf16[16,8832]{1,0:T(8,128)(2,1)S(1)}, u32[]{:S(2)}, u32[]{:S(2)}) collective-permute-start(bf16[16,8832]{1,0:T(8,128)(2,1)S(1)} %collective-permute-done.3.refs_6_), channel_id=1, source_target_pairs={{0,4},{4,0},{8,12},{12,8},{16,20},{20,16},{24,28},{28,24},{1,5},{5... | collective-permute-start | bytes 847880 | tf_op jit(solution)/shard_map/ppermute | solution.py:25
  28.8 1.4 %collective-permute-start.7 = (f32[4,2,16,256]{3,2,1,0:T(8,128)S(1)}, f32[4,2,16,256]{3,2,1,0:T(8,128)S(1)}, u32[]{:S(2)}, u32[]{:S(2)}) collective-permute-start(f32[4,2,16,256]{3,2,1,0:T(8,128)S(1)} %get-tuple-element.27), channel_id=1, source_target_pairs={{0,4},{4,0},{8,12},{12,8},{16,20},{20,16},{24,28},{28,24},{1,5},{5... | collective-permute-start | bytes 393224 | tf_op jit(solution)/shard_map/ppermute | solution.py:25
  30.2 4.1 %collective-permute-start.8 = (f32[2,16,256]{2,1,0:T(8,128)S(1)}, f32[2,16,256]{2,1,0:T(8,128)S(1)}, u32[]{:S(2)}, u32[]{:S(2)}) collective-permute-start(f32[2,16,256]{2,1,0:T(8,128)S(1)} %get-tuple-element.28), channel_id=1, source_target_pairs={{0,8},{4,12},{8,0},{12,4},{16,24},{20,28},{24,16},{28,20},{1,9},{5... | collective-permute-start | bytes 98312 | tf_op jit(solution)/shard_map/ppermute | solution.py:25
  31.1 5.5 %collective-permute-start.10 = (f32[2,16,256]{2,1,0:T(8,128)S(1)}, f32[2,16,256]{2,1,0:T(8,128)S(1)}, u32[]{:S(2)}, u32[]{:S(2)}) collective-permute-start(f32[2,16,256]{2,1,0:T(8,128)S(1)} %get-tuple-element.29), channel_id=1, source_target_pairs={{0,24},{4,28},{8,16},{12,20},{16,8},{20,12},{24,0},{28,4},{1,25},{... | collective-permute-start | bytes 98312 | tf_op jit(solution)/shard_map/ppermute | solution.py:25
  34.3 3.9 %collective-permute-start.9 = (f32[2,16,256]{2,1,0:T(8,128)S(1)}, f32[2,16,256]{2,1,0:T(8,128)S(1)}, u32[]{:S(2)}, u32[]{:S(2)}) collective-permute-start(f32[2,16,256]{2,1,0:T(8,128)S(1)} %get-tuple-element.30), channel_id=1, source_target_pairs={{0,16},{4,20},{8,24},{12,28},{16,0},{20,4},{24,8},{28,12},{1,17},{... | collective-permute-start | bytes 98312 | tf_op jit(solution)/shard_map/ppermute | solution.py:25
  38.3 7.4 %collective-permute-start.13 = (f32[2,16,256]{2,1,0:T(8,128)S(1)}, f32[2,16,256]{2,1,0:T(8,128)S(1)}, u32[]{:S(2)}, u32[]{:S(2)}) collective-permute-start(f32[2,16,256]{2,1,0:T(8,128)S(1)} %fusion.2), channel_id=1, source_target_pairs={{0,3},{1,2},{2,1},{3,0},{4,7},{5,6},{6,5},{7,4},{8,11},{9,10},{10,... | collective-permute-start | bytes 98312 | tf_op jit(solution)/shard_map/ppermute | solution.py:25
  42.1 4.8 %collective-permute-start.12 = (f32[2,16,256]{2,1,0:T(8,128)S(1)}, f32[2,16,256]{2,1,0:T(8,128)S(1)}, u32[]{:S(2)}, u32[]{:S(2)}) collective-permute-start(f32[2,16,256]{2,1,0:T(8,128)S(1)} %fusion.2), channel_id=1, source_target_pairs={{0,2},{1,3},{2,0},{3,1},{4,6},{5,7},{6,4},{7,5},{8,10},{9,11},{10,... | collective-permute-start | bytes 98312 | tf_op jit(solution)/shard_map/ppermute | solution.py:25
  42.4 4.5 %collective-permute-start.11 = (f32[2,16,256]{2,1,0:T(8,128)S(1)}, f32[2,16,256]{2,1,0:T(8,128)S(1)}, u32[]{:S(2)}, u32[]{:S(2)}) collective-permute-start(f32[2,16,256]{2,1,0:T(8,128)S(1)} %fusion.2), channel_id=1, source_target_pairs={{0,1},{1,0},{2,3},{3,2},{4,5},{5,4},{6,7},{7,6},{8,9},{9,8},{10,11... | collective-permute-start | bytes 98312 | tf_op jit(solution)/shard_map/ppermute | solution.py:25

commit v2 on v1

--- a/solution.py
+++ b/solution.py
@@ -26,43 +26,42 @@
 
 
 class Plan:
-    def __init__(self, group_tiles, fan_one, own, fan_two, zero_tile):
+    def __init__(self, group_tiles, fan_one, own, fan_two):
         self.group_tiles, self.fan_one, self.own, self.fan_two = group_tiles, fan_one, own, fan_two
         self.entries = own * fan_two
         self.dense = self.entries == group_tiles
         self.slots = group_tiles if self.dense else self.entries + own
         self.steps = -(-self.slots // BATCH)
         self.padded = self.steps * BATCH
-        self.place = 1
-        self.cols_two = self.place + group_tiles
-        self.count_two = self.cols_two + self.entries
-        self.cols_one = self.count_two + own
-        self.count_one = self.cols_one + group_tiles * fan_one
         self.tile_at = HEAD
         self.slot_at = self.tile_at + self.padded + BATCH
         self.column_at = self.slot_at + self.padded + BATCH
         self.entry_at = self.column_at + (self.padded + BATCH) * fan_one
         self.table = self.entry_at + self.entries
-        self.zero_tile = zero_tile
 
 
 def prepare_kernel(
-    plan, ints, bias_ref, adj_one_ref, adj_two_ref, w_ref, cot_ref,
+    plan, place_ref, cols_two_ref, count_two_ref, cols_one_ref, count_one_ref, bias_ref,
+    adj_one_ref, adj_two_ref, w_ref, cot_ref,
     d_ref, adj_one, adj_two, w_two, bias, table,
-    cot, back, inverse, active, sems, adj_sems,
+    cot, back, place, cols_two, count_two, cols_one, count_one, inverse, active, sems, adj_sems,
 ):
     own, fan, fan_one = plan.own, plan.fan_two, plan.fan_one
     tile = adj_two.shape[-1]
     hidden = w_two.shape[-1]
-    first = ints[0] * own
+    first = lax.axis_index("feat") * own
     own_slot = first if plan.dense else plan.entries
 
-    copies = [
-        pltpu.make_async_copy(source, to, sems.at[i])
-        for i, (source, to) in enumerate(((w_ref, w_two), (cot_ref, cot), (adj_two_ref, adj_two)))
-    ]
+    pairs = (
+        (place_ref, place), (cols_two_ref, cols_two), (count_two_ref, count_two),
+        (cols_one_ref, cols_one), (count_one_ref, count_one),
+        (w_ref, w_two), (cot_ref, cot), (adj_two_ref, adj_two),
+    )
+    copies = [pltpu.make_async_copy(source, to, sems.at[i]) for i, (source, to) in enumerate(pairs)]
     for copy in copies:
         copy.start()
+    for copy in copies[:5]:
+        copy.wait()
 
     def adj_copy(i):
         t = table[plan.tile_at + i]
@@ -70,14 +69,14 @@
 
     @pl.loop(0, plan.group_tiles, unroll=8)
     def _(t):
-        inverse[ints[plan.place + t]] = t
+        inverse[place[0, t]] = t
 
     @pl.loop(0, own)
     def _(p):
-        count = ints[plan.count_two + p]
+        count = count_two[0, p]
         for k in range(fan):
             e = p * fan + k
-            slot = ints[plan.cols_two + e] if plan.dense else e
+            slot = cols_two[p, k] if plan.dense else e
             live = k < count
             table[plan.entry_at + e] = jnp.where(live, slot, own_slot)
             if plan.dense:
@@ -91,7 +90,8 @@
         if plan.dense:
             placed = s
         else:
-            named = ints[plan.cols_two + jnp.minimum(s, plan.entries - 1)]
+            e = jnp.minimum(s, plan.entries - 1)
+            named = cols_two[lax.div(e, fan), lax.rem(e, fan)]
             placed = jnp.where(s < plan.entries, named, first + s - plan.entries)
         table[plan.tile_at + n] = inverse[placed]
         table[plan.slot_at + n] = s
@@ -112,10 +112,8 @@
         for b in range(BATCH):
             i = step * BATCH + b
             t = table[plan.tile_at + i]
-            count = ints[plan.count_one + t]
             for k in range(fan_one):
-                column = ints[plan.cols_one + t * fan_one + k]
-                table[plan.column_at + i * fan_one + k] = jnp.where(k < count, column, plan.zero_tile)
+                table[plan.column_at + i * fan_one + k] = cols_one[k, t]
 
     @pl.loop(0, steps)
     def _(step):
@@ -127,16 +125,16 @@
     if not plan.dense:
         for p in range(own):
             d_ref[plan.entries + p] = jnp.zeros((hidden, tile), d_ref.dtype)
-    bias[...] = jnp.broadcast_to(bias_ref[...], (tile, hidden)).T
-
-    copies[0].wait()
-    copies[1].wait()
+    bias[...] = jnp.broadcast_to(0.5 * bias_ref[...], (tile, hidden)).T
+
+    copies[5].wait()
+    copies[6].wait()
     back[...] = dot(w_two[1], cot[...], NT).astype(back.dtype)
-    copies[2].wait()
+    copies[7].wait()
 
     @pl.loop(0, own)
     def _(p):
-        @pl.loop(ints[plan.count_two + p], fan)
+        @pl.loop(count_two[0, p], fan)
         def _(k):
             adj_two[p, k] = jnp.zeros((tile, tile), adj_two.dtype)
 
@@ -145,7 +143,7 @@
         term = dot(back[:, p * tile : (p + 1) * tile], tiles).astype(d_ref.dtype)
         for k in range(fan):
             e = p * fan + k
-            slot = ints[plan.cols_two + e] if plan.dense else e
+            slot = cols_two[p, k] if plan.dense else e
             d_ref[slot] = term[:, k * tile : (k + 1) * tile]
 
     self_rows = dot(w_two[0], cot[...], NT)
@@ -156,7 +154,12 @@
     @pl.loop(0, steps)
     def _(step):
         for b in range(BATCH):
-            adj_copy(step * BATCH + b).wait()
+            i = step * BATCH + b
+            adj_copy(i).wait()
+
+            @pl.loop(count_one[0, table[plan.tile_at + i]], fan_one)
+            def _(k):
+                adj_one[i, k] = jnp.zeros((tile, tile), adj_one.dtype)
 
 
 def layer_one_kernel(plan, blocks, table, *refs):
@@ -191,10 +194,10 @@
         for b in range(0, BATCH, 2):
             z = dot(weight[...], both[at, :, b * tile : (b + 2) * tile])
             for c in range(2):
-                v = z[:, lanes(c)] + bias[...]
-                s = 0.5 * jnp.tanh(0.5 * v) + 0.5
-                h = v * s
-                slope = s + h * (1.0 - s)
+                u = z[:, lanes(c)] + bias[...]
+                t = jnp.tanh(u)
+                h = u * (1.0 + t)
+                slope = (1.0 + t) + h * (1.0 - t)
                 slot = table[plan.slot_at + step * BATCH + b + c]
                 h_ref[slot] = h.astype(h_ref.dtype)
                 down = d_ref[slot].astype(jnp.float32) * slope
@@ -207,7 +210,7 @@
     for part in range(2):
         at = pl.ds(plan.group_tiles * tile + part * hidden, hidden)
         w = jnp.concatenate([x[:, at] for x in x_refs], axis=0)
-        weight[:, part * features : (part + 1) * features] = w.astype(jnp.float32).T.astype(weight.dtype)
+        weight[:, part * features : (part + 1) * features] = (0.5 * w.astype(jnp.float32)).T.astype(weight.dtype)
     total[...] = jnp.zeros_like(total)
     both[1] = jnp.zeros(both.shape[1:], both.dtype)
     downs[1] = jnp.zeros(downs.shape[1:], downs.dtype)
@@ -226,7 +229,7 @@
         out = even_ref if m % 2 == 0 else odd_ref
         for part in range(2):
             at = part * features + m * share
-            out[m // 2, part] = total[at : at + share]
+            out[m // 2, part] = 0.5 * total[at : at + share]
 
 
 def layer_two_kernel(plan, table, h_ref, adj_two, w_ref, out_ref, agg, out, sems):
@@ -249,6 +252,9 @@
 
 
 def call_prepare(plan, ints, bias, adj_one, adj_two, w_two, cot):
+    adj_one, adj_two, w_two, cot, *ints = [
+        pltpu.with_memory_space_constraint(a, pltpu.HBM) for a in (adj_one, adj_two, w_two, cot, *ints)
+    ]
     own, fan, tile, _ = adj_two.shape
     hidden = w_two.shape[-1]
     kind = adj_one.dtype
@@ -262,14 +268,15 @@
             jax.ShapeDtypeStruct((hidden, tile), jnp.float32),
             jax.ShapeDtypeStruct((plan.table,), jnp.int32),
         ),
-        in_specs=[SMEM, VMEM] + [HBM] * 4,
+        in_specs=[HBM] * 5 + [VMEM] + [HBM] * 4,
         out_specs=(VMEM,) * 5 + (SMEM,),
         scratch_shapes=[
             pltpu.VMEM((own * tile, hidden), kind),
             pltpu.VMEM((hidden, own * tile), kind),
+            *[pltpu.SMEM(a.shape, jnp.int32) for a in ints],
             pltpu.SMEM((plan.group_tiles,), jnp.int32),
             pltpu.SMEM((plan.slots,), jnp.int32),
-            pltpu.SemaphoreType.DMA((3,)),
+            pltpu.SemaphoreType.DMA((8,)),
             pltpu.SemaphoreType.DMA((plan.padded,)),
         ],
         compiler_params=pltpu.CompilerParams(vmem_limit_bytes=34 << 20),
@@ -277,7 +284,7 @@
             flops=2 * plan.entries * tile * tile * hidden, bytes_accessed=20 << 20, transcendentals=0
         ),
         name="prepare",
-    )(ints, bias, adj_one, adj_two, w_two, cot)
+    )(*ints, bias, adj_one, adj_two, w_two, cot)
 
 
 def call_layer_one(plan, feat_count, table, gathered, bias, adj_one, down):
@@ -350,18 +357,13 @@
     own, fan_two = adj_two.shape[1:3]
     hidden = w_two.shape[-1]
     feat_count = lax.axis_size("feat")
-    plan = Plan(place.shape[1], adj_one.shape[2], own, fan_two, place.shape[1] + 2 * hidden // tile)
-
-    nothing = jnp.zeros((feat_dev, tile), x_local.dtype)
-    packed = jnp.concatenate([x_local, w_one[0], w_one[1], nothing], axis=1)
+    plan = Plan(place.shape[1], adj_one.shape[2], own, fan_two)
+
+    packed = jnp.concatenate([x_local, w_one[0], w_one[1]], axis=1)
     near = [packed] + [exchange(packed, "feat", m) for m in range(2, feat_count, 2)]
     far = [exchange(packed, "feat", 1)]
 
-    me = lax.axis_index("feat").astype(jnp.int32).reshape(1)
-    ints = jnp.concatenate(
-        [me]
-        + [a.reshape(-1) for a in (place, cols_two, count_two, cols_one, count_one)]
-    )
+    ints = (place, cols_two[0], count_two, cols_one[0].T, count_one)
     down, adj_near, adj_far, weights, bias, table = call_prepare(
         plan, ints, bias_one.astype(jnp.float32).reshape(1, hidden), adj_one[0], adj_two[0], w_two, cotangent[0]
     )

time: 47.9 us -> 45.6 us (0.952)
  local copies, waits for them, and re-layouts: 6.73 us -> 0.73 us
  waiting for transfers between devices: 8.01 us -> 10.9 us
  Pallas kernels: 15.6 us -> 17.3 us
  starting transfers between devices: 14.2 us -> 13.2 us
    unnamed x7 -> x0, local copies, waits for them, and re-layouts: 4.35 us -> none
    ppermute x14, waiting for transfers between devices: 8.01 us -> 10.9 us  [exchange(): return lax.ppermute(array, axis, [(i, i ^ mask) for i in range(size)])]
    ppermute x14, starting transfers between devices: 14.2 us -> 13.2 us  [exchange(): return lax.ppermute(array, axis, [(i, i ^ mask) for i in range(size)])]
    pallas_call x1, Pallas kernels: 6.56 us -> 7.52 us  [call_layer_one(): pl.pallas_call(functools.partial(layer_one_kernel, plan, blocks), out_sha...]
    reshape x2 -> x0, local copies, waits for them, and re-layouts: 0.87 us -> none  [body(): a.reshape(-1)]
    pallas_call x1, Pallas kernels: 6.07 us -> 6.88 us  [call_prepare(): pl.pallas_call(functools.partial(prepare_kernel, plan), out_shape=(jax.Sh...]
    concatenate x2 -> x0, local copies, waits for them, and re-layouts: 0.78 us -> none  [the longest x1 0.77 us: body(): jnp.concatenate([me] + [a.reshape(-1) for a in (place, cols_two, count_tw...]
  transfers between devices with their start and end apart: 14 -> 14, of which waited for: 7 -> 10; matrix products, arithmetic and copies ran while one was open for 6% -> 1% of each run, Pallas kernels for 19% -> 22%
where the time goes in v2:
time: 45.6 us; the launch traced here: 45.2 us
  Pallas kernels  17.3 us (38%)
  starting transfers between devices  13.2 us (29%)
  waiting for transfers between devices  10.9 us (24%)
  other arithmetic  2.28 us (5%)
  local copies, waits for them, and re-layouts  0.73 us (2%)
  between operations  0.71 us (2%)
    ppermute x14, starting transfers between devices, exchange(): return lax.ppermute(array, axis, [(i, i ^ mask) for i in range(size)])  13.2 us
    ppermute x14, waiting for transfers between devices, exchange(): return lax.ppermute(array, axis, [(i, i ^ mask) for i in range(size)])  10.9 us
    pallas_call x1, Pallas kernels, call_layer_one(): pl.pallas_call(functools.partial(layer_one_kernel, plan, blocks), out_sha...  7.52 us
    pallas_call x1, Pallas kernels, call_prepare(): pl.pallas_call(functools.partial(prepare_kernel, plan), out_shape=(jax.Sh...  6.88 us
    pallas_call x1, Pallas kernels, call_layer_two(): pl.pallas_call(functools.partial(layer_two_kernel, plan), out_shape=jax.S...  2.93 us
    concatenate x1, other arithmetic, body(): packed = jnp.concatenate([x_local, w_one[0], w_one[1]], axis=1)  0.97 us
  transfers between devices with their start and end apart: 14, of which 10 were waited for; matrix products, arithmetic and copies ran while one was open for 1% of the time, Pallas kernels for 22%

profile of v2, /device:TPU:0, one launch (start us, length us, event | category | flops | bytes accessed | tf_op | source)
XLA Modules:
  0.0 45.2 jit_solution(9176113558341408575)
XLA Ops:
  0.6 0.7 %slice_bitcast_fusion.5 = (bf16[16,256]{1,0:T(8,128)(2,1)S(1)}, bf16[16,256]{1,0:T(8,128)(2,1)S(1)}) fusion(bf16[2,16,256]{2,1,0:T(8,128)(2,1)} %param.17), kind=kLoop, calls=%fused_computation.10 | loop fusion | bytes 32768 | tf_op jit(solution)/shard_map/squeeze | solution.py:362
  1.3 1.0 %pad_maximum_fusion.refs_0_ = bf16[16,8704]{1,0:T(8,128)(2,1)S(1)} fusion(bf16[16,256]{1,0:T(8,128)(2,1)S(1)} %get-tuple-element.32, bf16[16,256]{1,0:T(8,128)(2,1)S(1)} %get-tuple-element.31, bf16[16,8192]{1,0:T(8,128)(2,1)} %bitcast.33), kind=kLoop, calls=%fused_computation | loop fusion | flops 835584 | bytes 557056 | tf_op jit(solution)/shard_map/concatenate | solution.py:362
  2.3 4.0 %collective-permute-start.3 = (bf16[16,8704]{1,0:T(8,128)(2,1)S(1)}, bf16[16,8704]{1,0:T(8,128)(2,1)S(1)}, u32[]{:S(2)}, u32[]{:S(2)}) collective-permute-start(bf16[16,8704]{1,0:T(8,128)(2,1)S(1)} %pad_maximum_fusion.refs_0_), channel_id=1, source_target_pairs={{0,24},{4,28},{8,16},{12,20},{16,8},{20,12},{24,0},{28,4},{1,25},{... | collective-permute-start | bytes 835592 | tf_op jit(solution)/shard_map/ppermute | solution.py:25
  6.3 0.5 %collective-permute-start.2 = (bf16[16,8704]{1,0:T(8,128)(2,1)S(1)}, bf16[16,8704]{1,0:T(8,128)(2,1)S(1)}, u32[]{:S(2)}, u32[]{:S(2)}) collective-permute-start(bf16[16,8704]{1,0:T(8,128)(2,1)S(1)} %pad_maximum_fusion.refs_0_), channel_id=1, source_target_pairs={{0,16},{4,20},{8,24},{12,28},{16,0},{20,4},{24,8},{28,12},{1,17},{... | collective-permute-start | bytes 835592 | tf_op jit(solution)/shard_map/ppermute | solution.py:25
  6.8 0.1 collective-permute-start.1
  6.9 0.0 collective-permute-start
  6.9 0.7 %reshape.15 = f32[256]{0:T(256)S(1)} convert(bf16[256]{0:T(256)(128)(2,1)} %param.18) | non-fusion elementwise | flops 256 | bytes 1536 | tf_op jit(solution)/shard_map/reshape | solution.py:368
  7.6 6.9 %prepare.1 = (bf16[68,256,128]{2,1,0:T(8,128)(2,1)S(1)}, bf16[64,4,128,128]{3,2,1,0:T(8,128)(2,1)S(1)}, bf16[8,8,128,128]{3,2,1,0:T(8,128)(2,1)S(1)}, bf16[2,256...) custom-call(s32[1,64]{1,0:T(1,128)} %place_ref.1, s32[8,8]{1,0:T(8,128)} %bitcast.34, ...), custom_call_target="tpu_custom_call" | custom-call | flops 536870912 | bytes 20971520 | tf_op jit(solution)/shard_map/prepare/pallas_call | solution.py:261
  14.5 0.0 collective-permute-done.3.refs_6_
  14.5 4.4 %collective-permute-done.2.refs_4_ = bf16[16,8704]{1,0:T(8,128)(2,1)S(1)} collective-permute-done((bf16[16,8704]{1,0:T(8,128)(2,1)S(1)}, bf16[16,8704]{1,0:T(8,128)(2,1)S(1)}, u32[]{:S(2)}, u32[]{:S(2)}) %collective-permute-start.2) | collective-permute-done | bytes 278560 | tf_op jit(solution)/shard_map/ppermute | solution.py:25
  18.9 0.3 collective-permute-done.1.refs_2_
  19.2 0.0 collective-permute-start.4
  19.2 0.5 %collective-permute-start.5 = (bf16[16,8704]{1,0:T(8,128)(2,1)S(1)}, bf16[16,8704]{1,0:T(8,128)(2,1)S(1)}, u32[]{:S(2)}, u32[]{:S(2)}) collective-permute-start(bf16[16,8704]{1,0:T(8,128)(2,1)S(1)} %collective-permute-done.2.refs_4_), channel_id=1, source_target_pairs={{0,4},{4,0},{8,12},{12,8},{16,20},{20,16},{24,28},{28,24},{1,5},{5... | collective-permute-start | bytes 835592 | tf_op jit(solution)/shard_map/ppermute | solution.py:25
  19.7 0.0 collective-permute-start.6
  19.7 0.0 collective-permute-done.refs_1_
  19.7 1.0 %collective-permute-done.4.refs_3_ = bf16[16,8704]{1,0:T(8,128)(2,1)S(1)} collective-permute-done((bf16[16,8704]{1,0:T(8,128)(2,1)S(1)}, bf16[16,8704]{1,0:T(8,128)(2,1)S(1)}, u32[]{:S(2)}, u32[]{:S(2)}) %collective-permute-start.4) | collective-permute-done | bytes 278560 | tf_op jit(solution)/shard_map/ppermute | solution.py:25
  20.8 0.4 collective-permute-done.5.refs_5_
  21.2 0.4 collective-permute-done.6.refs_7_
  21.6 7.5 %layer_one.1 = (f32[4,2,16,256]{3,2,1,0:T(8,128)S(1)}, f32[4,2,16,256]{3,2,1,0:T(8,128)S(1)}, bf16[68,256,128]{2,1,0:T(8,128)(2,1)S(1)}) custom-call(s32[480]{0:T(512)S(1)} %get-tuple-element.15.table, bf16[16,8704]{1,0:T(8,128)(2,1)S(1)} %pad_maximum_fusion.refs_0_, bf16[16,8704]{1,0:T(8,128)(2,1)S(1)} %collective-permute-done.refs_1_, ...), custom_call_target="tpu_custom_call" | custom-call | flops 3221225472 | bytes 20971520 | tf_op jit(solution)/shard_map/layer_one/pallas_call | solution.py:297
  29.1 0.1 collective-permute-start.7
  29.2 1.3 %collective-permute-done.7 = f32[4,2,16,256]{3,2,1,0:T(8,128)S(1)} collective-permute-done((f32[4,2,16,256]{3,2,1,0:T(8,128)S(1)}, f32[4,2,16,256]{3,2,1,0:T(8,128)S(1)}, u32[]{:S(2)}, u32[]{:S(2)}) %collective-permute-start.7) | collective-permute-done | bytes 131104 | tf_op jit(solution)/shard_map/ppermute | solution.py:25
  30.5 0.1 collective-permute-start.8
  30.6 1.4 %collective-permute-start.10 = (f32[2,16,256]{2,1,0:T(8,128)S(1)}, f32[2,16,256]{2,1,0:T(8,128)S(1)}, u32[]{:S(2)}, u32[]{:S(2)}) collective-permute-start(f32[2,16,256]{2,1,0:T(8,128)S(1)} %get-tuple-element.29), channel_id=1, source_target_pairs={{0,24},{4,28},{8,16},{12,20},{16,8},{20,12},{24,0},{28,4},{1,25},{... | collective-permute-start | bytes 98312 | tf_op jit(solution)/shard_map/ppermute | solution.py:25
  32.0 2.1 %collective-permute-start.9 = (f32[2,16,256]{2,1,0:T(8,128)S(1)}, f32[2,16,256]{2,1,0:T(8,128)S(1)}, u32[]{:S(2)}, u32[]{:S(2)}) collective-permute-start(f32[2,16,256]{2,1,0:T(8,128)S(1)} %get-tuple-element.30), channel_id=1, source_target_pairs={{0,16},{4,20},{8,24},{12,28},{16,0},{20,4},{24,8},{28,12},{1,17},{... | collective-permute-start | bytes 98312 | tf_op jit(solution)/shard_map/ppermute | solution.py:25
  34.1 0.7 %collective-permute-done.8 = f32[2,16,256]{2,1,0:T(8,128)S(1)} collective-permute-done((f32[2,16,256]{2,1,0:T(8,128)S(1)}, f32[2,16,256]{2,1,0:T(8,128)S(1)}, u32[]{:S(2)}, u32[]{:S(2)}) %collective-permute-start.8) | collective-permute-done | bytes 32800 | tf_op jit(solution)/shard_map/ppermute | solution.py:25
  34.8 0.7 %collective-permute-done.10 = f32[2,16,256]{2,1,0:T(8,128)S(1)} collective-permute-done((f32[2,16,256]{2,1,0:T(8,128)S(1)}, f32[2,16,256]{2,1,0:T(8,128)S(1)}, u32[]{:S(2)}, u32[]{:S(2)}) %collective-permute-start.10) | collective-permute-done | bytes 32800 | tf_op jit(solution)/shard_map/ppermute | solution.py:25
  35.5 0.5 %collective-permute-done.9 = f32[2,16,256]{2,1,0:T(8,128)S(1)} collective-permute-done((f32[2,16,256]{2,1,0:T(8,128)S(1)}, f32[2,16,256]{2,1,0:T(8,128)S(1)}, u32[]{:S(2)}, u32[]{:S(2)}) %collective-permute-start.9) | collective-permute-done | bytes 32800 | tf_op jit(solution)/shard_map/ppermute | solution.py:25
  36.0 3.7 %collective-permute-start.13 = (f32[2,16,256]{2,1,0:T(8,128)S(1)}, f32[2,16,256]{2,1,0:T(8,128)S(1)}, u32[]{:S(2)}, u32[]{:S(2)}) collective-permute-start(f32[2,16,256]{2,1,0:T(8,128)S(1)} %fusion.2), channel_id=1, source_target_pairs={{0,3},{1,2},{2,1},{3,0},{4,7},{5,6},{6,5},{7,4},{8,11},{9,10},{10,... | collective-permute-start | bytes 98312 | tf_op jit(solution)/shard_map/ppermute | solution.py:25
  39.7 0.0 collective-permute-start.12
  39.7 0.7 %collective-permute-start.11 = (f32[2,16,256]{2,1,0:T(8,128)S(1)}, f32[2,16,256]{2,1,0:T(8,128)S(1)}, u32[]{:S(2)}, u32[]{:S(2)}) collective-permute-start(f32[2,16,256]{2,1,0:T(8,128)S(1)} %fusion.2), channel_id=1, source_target_pairs={{0,1},{1,0},{2,3},{3,2},{4,5},{5,4},{6,7},{7,6},{8,9},{9,8},{10,11... | collective-permute-start | bytes 98312 | tf_op jit(solution)/shard_map/ppermute | solution.py:25
  40.5 2.9 %layer_two.1 = bf16[8,128,256]{2,1,0:T(8,128)(2,1)} custom-call(s32[480]{0:T(512)S(1)} %get-tuple-element.15.table, bf16[68,256,128]{2,1,0:T(8,128)(2,1)S(1)} %get-tuple-element.23.h_ref, bf16[8,8,128,128]{3,2,1,0:T(8,128)(2,1)S(1)} %get-tuple-element.24.adj_two, bf16[2,256,256]{2,1,0:T(8,128)(2,1)S(1)} %get-tuple-element.25.w_ref), custom_call_target="tpu_custom_call" | custom-call | flops 536870912 | bytes 8388608 | tf_op jit(solution)/shard_map/layer_two/pallas_call | solution.py:322
  43.4 0.0 collective-permute-done.13
  43.4 1.2 %collective-permute-done.12 = f32[2,16,256]{2,1,0:T(8,128)S(1)} collective-permute-done((f32[2,16,256]{2,1,0:T(8,128)S(1)}, f32[2,16,256]{2,1,0:T(8,128)S(1)}, u32[]{:S(2)}, u32[]{:S(2)}) %collective-permute-start.12) | collective-permute-done | bytes 32800 | tf_op jit(solution)/shard_map/ppermute | solution.py:25
  44.6 0.0 collective-permute-done.11
  44.6 0.6 %add_add_fusion = f32[2,16,256]{2,1,0:T(8,128)} fusion(f32[2,16,256]{2,1,0:T(8,128)S(1)} %collective-permute-done.12, f32[2,16,256]{2,1,0:T(8,128)S(1)} %collective-permute-done.13, f32[2,16,256]{2,1,0:T(8,128)S(1)} %fusion.2, f32[2,16,256]{2,1,0:T(8,128)S(1)} %collective-permute-done.11), kind=kLoop, calls=%fused_computation.8 | loop fusion | flops 24576 | bytes 163840 | tf_op jit(solution)/shard_map/add | solution.py:387
  (3 shorter events, 0.0 us)
Async XLA Ops:
  2.3 12.2 %collective-permute-start.3 = (bf16[16,8704]{1,0:T(8,128)(2,1)S(1)}, bf16[16,8704]{1,0:T(8,128)(2,1)S(1)}, u32[]{:S(2)}, u32[]{:S(2)}) collective-permute-start(bf16[16,8704]{1,0:T(8,128)(2,1)S(1)} %pad_maximum_fusion.refs_0_), channel_id=1, source_target_pairs={{0,24},{4,28},{8,16},{12,20},{16,8},{20,12},{24,0},{28,4},{1,25},{... | collective-permute-start | bytes 835592 | tf_op jit(solution)/shard_map/ppermute | solution.py:25
  6.3 12.6 %collective-permute-start.2 = (bf16[16,8704]{1,0:T(8,128)(2,1)S(1)}, bf16[16,8704]{1,0:T(8,128)(2,1)S(1)}, u32[]{:S(2)}, u32[]{:S(2)}) collective-permute-start(bf16[16,8704]{1,0:T(8,128)(2,1)S(1)} %pad_maximum_fusion.refs_0_), channel_id=1, source_target_pairs={{0,16},{4,20},{8,24},{12,28},{16,0},{20,4},{24,8},{28,12},{1,17},{... | collective-permute-start | bytes 835592 | tf_op jit(solution)/shard_map/ppermute | solution.py:25
  6.8 12.4 %collective-permute-start.1 = (bf16[16,8704]{1,0:T(8,128)(2,1)S(1)}, bf16[16,8704]{1,0:T(8,128)(2,1)S(1)}, u32[]{:S(2)}, u32[]{:S(2)}) collective-permute-start(bf16[16,8704]{1,0:T(8,128)(2,1)S(1)} %pad_maximum_fusion.refs_0_), channel_id=1, source_target_pairs={{0,8},{4,12},{8,0},{12,4},{16,24},{20,28},{24,16},{28,20},{1,9},{5... | collective-permute-start | bytes 835592 | tf_op jit(solution)/shard_map/ppermute | solution.py:25
  6.9 12.8 %collective-permute-start = (bf16[16,8704]{1,0:T(8,128)(2,1)S(1)}, bf16[16,8704]{1,0:T(8,128)(2,1)S(1)}, u32[]{:S(2)}, u32[]{:S(2)}) collective-permute-start(bf16[16,8704]{1,0:T(8,128)(2,1)S(1)} %pad_maximum_fusion.refs_0_), channel_id=1, source_target_pairs={{0,4},{4,0},{8,12},{12,8},{16,20},{20,16},{24,28},{28,24},{1,5},{5... | collective-permute-start | bytes 835592 | tf_op jit(solution)/shard_map/ppermute | solution.py:25
  19.2 1.6 %collective-permute-start.4 = (bf16[16,8704]{1,0:T(8,128)(2,1)S(1)}, bf16[16,8704]{1,0:T(8,128)(2,1)S(1)}, u32[]{:S(2)}, u32[]{:S(2)}) collective-permute-start(bf16[16,8704]{1,0:T(8,128)(2,1)S(1)} %collective-permute-done.1.refs_2_), channel_id=1, source_target_pairs={{0,4},{4,0},{8,12},{12,8},{16,20},{20,16},{24,28},{28,24},{1,5},{5... | collective-permute-start | bytes 835592 | tf_op jit(solution)/shard_map/ppermute | solution.py:25
  19.2 2.0 %collective-permute-start.5 = (bf16[16,8704]{1,0:T(8,128)(2,1)S(1)}, bf16[16,8704]{1,0:T(8,128)(2,1)S(1)}, u32[]{:S(2)}, u32[]{:S(2)}) collective-permute-start(bf16[16,8704]{1,0:T(8,128)(2,1)S(1)} %collective-permute-done.2.refs_4_), channel_id=1, source_target_pairs={{0,4},{4,0},{8,12},{12,8},{16,20},{20,16},{24,28},{28,24},{1,5},{5... | collective-permute-start | bytes 835592 | tf_op jit(solution)/shard_map/ppermute | solution.py:25
  19.7 1.8 %collective-permute-start.6 = (bf16[16,8704]{1,0:T(8,128)(2,1)S(1)}, bf16[16,8704]{1,0:T(8,128)(2,1)S(1)}, u32[]{:S(2)}, u32[]{:S(2)}) collective-permute-start(bf16[16,8704]{1,0:T(8,128)(2,1)S(1)} %collective-permute-done.3.refs_6_), channel_id=1, source_target_pairs={{0,4},{4,0},{8,12},{12,8},{16,20},{20,16},{24,28},{28,24},{1,5},{5... | collective-permute-start | bytes 835592 | tf_op jit(solution)/shard_map/ppermute | solution.py:25
  29.1 1.4 %collective-permute-start.7 = (f32[4,2,16,256]{3,2,1,0:T(8,128)S(1)}, f32[4,2,16,256]{3,2,1,0:T(8,128)S(1)}, u32[]{:S(2)}, u32[]{:S(2)}) collective-permute-start(f32[4,2,16,256]{3,2,1,0:T(8,128)S(1)} %get-tuple-element.27), channel_id=1, source_target_pairs={{0,4},{4,0},{8,12},{12,8},{16,20},{20,16},{24,28},{28,24},{1,5},{5... | collective-permute-start | bytes 393224 | tf_op jit(solution)/shard_map/ppermute | solution.py:25
  30.5 4.3 %collective-permute-start.8 = (f32[2,16,256]{2,1,0:T(8,128)S(1)}, f32[2,16,256]{2,1,0:T(8,128)S(1)}, u32[]{:S(2)}, u32[]{:S(2)}) collective-permute-start(f32[2,16,256]{2,1,0:T(8,128)S(1)} %get-tuple-element.28), channel_id=1, source_target_pairs={{0,8},{4,12},{8,0},{12,4},{16,24},{20,28},{24,16},{28,20},{1,9},{5... | collective-permute-start | bytes 98312 | tf_op jit(solution)/shard_map/ppermute | solution.py:25
  30.6 4.9 %collective-permute-start.10 = (f32[2,16,256]{2,1,0:T(8,128)S(1)}, f32[2,16,256]{2,1,0:T(8,128)S(1)}, u32[]{:S(2)}, u32[]{:S(2)}) collective-permute-start(f32[2,16,256]{2,1,0:T(8,128)S(1)} %get-tuple-element.29), channel_id=1, source_target_pairs={{0,24},{4,28},{8,16},{12,20},{16,8},{20,12},{24,0},{28,4},{1,25},{... | collective-permute-start | bytes 98312 | tf_op jit(solution)/shard_map/ppermute | solution.py:25
  32.0 4.0 %collective-permute-start.9 = (f32[2,16,256]{2,1,0:T(8,128)S(1)}, f32[2,16,256]{2,1,0:T(8,128)S(1)}, u32[]{:S(2)}, u32[]{:S(2)}) collective-permute-start(f32[2,16,256]{2,1,0:T(8,128)S(1)} %get-tuple-element.30), channel_id=1, source_target_pairs={{0,16},{4,20},{8,24},{12,28},{16,0},{20,4},{24,8},{28,12},{1,17},{... | collective-permute-start | bytes 98312 | tf_op jit(solution)/shard_map/ppermute | solution.py:25
  36.0 7.4 %collective-permute-start.13 = (f32[2,16,256]{2,1,0:T(8,128)S(1)}, f32[2,16,256]{2,1,0:T(8,128)S(1)}, u32[]{:S(2)}, u32[]{:S(2)}) collective-permute-start(f32[2,16,256]{2,1,0:T(8,128)S(1)} %fusion.2), channel_id=1, source_target_pairs={{0,3},{1,2},{2,1},{3,0},{4,7},{5,6},{6,5},{7,4},{8,11},{9,10},{10,... | collective-permute-start | bytes 98312 | tf_op jit(solution)/shard_map/ppermute | solution.py:25
  39.7 4.8 %collective-permute-start.12 = (f32[2,16,256]{2,1,0:T(8,128)S(1)}, f32[2,16,256]{2,1,0:T(8,128)S(1)}, u32[]{:S(2)}, u32[]{:S(2)}) collective-permute-start(f32[2,16,256]{2,1,0:T(8,128)S(1)} %fusion.2), channel_id=1, source_target_pairs={{0,2},{1,3},{2,0},{3,1},{4,6},{5,7},{6,4},{7,5},{8,10},{9,11},{10,... | collective-permute-start | bytes 98312 | tf_op jit(solution)/shard_map/ppermute | solution.py:25
  39.7 4.8 %collective-permute-start.11 = (f32[2,16,256]{2,1,0:T(8,128)S(1)}, f32[2,16,256]{2,1,0:T(8,128)S(1)}, u32[]{:S(2)}, u32[]{:S(2)}) collective-permute-start(f32[2,16,256]{2,1,0:T(8,128)S(1)} %fusion.2), channel_id=1, source_target_pairs={{0,1},{1,0},{2,3},{3,2},{4,5},{5,4},{6,7},{7,6},{8,9},{9,8},{10,11... | collective-permute-start | bytes 98312 | tf_op jit(solution)/shard_map/ppermute | solution.py:25

commit v3 on v2

--- a/solution.py
+++ b/solution.py
@@ -31,7 +31,8 @@
         self.entries = own * fan_two
         self.dense = self.entries == group_tiles
         self.slots = group_tiles if self.dense else self.entries + own
-        self.steps = -(-self.slots // BATCH)
+        self.few = fan_one // 2
+        self.steps = -(-self.slots // BATCH) + 1
         self.padded = self.steps * BATCH
         self.tile_at = HEAD
         self.slot_at = self.tile_at + self.padded + BATCH
@@ -86,26 +87,38 @@
         if not plan.dense:
             active[plan.entries + p] = 1
 
-    def visit(s, n):
+    def pad(start, end):
+        @pl.loop(start, end)
+        def _(i):
+            table[plan.tile_at + i] = 0
+            table[plan.slot_at + i] = plan.slots + lax.rem(i, BATCH)
+
+    def whole_steps(n):
+        return lax.div(n + BATCH - 1, BATCH)
+
+    def visit(few, s, n):
         if plan.dense:
             placed = s
         else:
             e = jnp.minimum(s, plan.entries - 1)
             named = cols_two[lax.div(e, fan), lax.rem(e, fan)]
             placed = jnp.where(s < plan.entries, named, first + s - plan.entries)
-        table[plan.tile_at + n] = inverse[placed]
+        t = inverse[placed]
+        table[plan.tile_at + n] = t
         table[plan.slot_at + n] = s
-        return n + active[s]
-
-    n = lax.fori_loop(0, plan.slots, visit, jnp.int32(0), unroll=8)
-    steps = lax.div(n + BATCH - 1, BATCH)
+        count = count_one[0, t]
+        fits = count <= plan.few if few else count > plan.few
+        return n + jnp.where(fits, active[s], 0)
+
+    n = lax.fori_loop(0, plan.slots, functools.partial(visit, True), jnp.int32(0), unroll=8)
+    few_steps = whole_steps(n)
+    pad(n, few_steps * BATCH)
+    n = lax.fori_loop(0, plan.slots, functools.partial(visit, False), few_steps * BATCH, unroll=8)
+    steps = whole_steps(n)
+    pad(n, plan.padded + BATCH)
     table[0] = steps
     table[1] = own_slot
-
-    @pl.loop(n, plan.padded + BATCH)
-    def _(i):
-        table[plan.tile_at + i] = 0
-        table[plan.slot_at + i] = plan.slots + lax.rem(i, BATCH)
+    table[2] = few_steps
 
     @pl.loop(0, steps + 1)
     def _(step):
@@ -165,7 +178,6 @@
 def layer_one_kernel(plan, blocks, table, *refs):
     x_refs = refs[:blocks]
     bias, adj_one, d_ref, even_ref, odd_ref, h_ref, weight, total, both, downs = refs[blocks:]
-    fan = plan.fan_one
     tile = adj_one.shape[-1]
     hidden = bias.shape[0]
     features = x_refs[0].shape[0] * blocks
@@ -178,12 +190,12 @@
     def lanes(b):
         return slice(b * tile, (b + 1) * tile)
 
-    def aggregate(step):
+    def aggregate(step, fan):
         at = lax.rem(step, 2)
         for b in range(BATCH):
             i = step * BATCH + b
             j = jnp.minimum(i, plan.padded - 1)
-            x_all = [x_tile(table[plan.column_at + i * fan + k]) for k in range(fan)]
+            x_all = [x_tile(table[plan.column_at + i * plan.fan_one + k]) for k in range(fan)]
             tiles = [adj_one[j, k] for k in range(fan)]
             agg = dot(jnp.concatenate(x_all, axis=1), jnp.concatenate(tiles, axis=1), NT)
             both[at, :features, lanes(b)] = x_tile(table[plan.tile_at + i])
@@ -214,13 +226,20 @@
     total[...] = jnp.zeros_like(total)
     both[1] = jnp.zeros(both.shape[1:], both.dtype)
     downs[1] = jnp.zeros(downs.shape[1:], downs.dtype)
-    aggregate(0)
-
-    @pl.loop(0, steps)
+    aggregate(0, plan.fan_one)
+    turn = jnp.maximum(table[2] - 1, 0)
+
+    @pl.loop(0, turn)
     def _(step):
         contract(step - 1)
         activate(step)
-        aggregate(step + 1)
+        aggregate(step + 1, plan.few)
+
+    @pl.loop(turn, steps)
+    def _(step):
+        contract(step - 1)
+        activate(step)
+        aggregate(step + 1, plan.fan_one)
 
     contract(steps - 1)
     half = even_ref.shape[0]
@@ -280,9 +299,7 @@
             pltpu.SemaphoreType.DMA((plan.padded,)),
         ],
         compiler_params=pltpu.CompilerParams(vmem_limit_bytes=34 << 20),
-        cost_estimate=pl.CostEstimate(
-            flops=2 * plan.entries * tile * tile * hidden, bytes_accessed=20 << 20, transcendentals=0
-        ),
+        cost_estimate=pl.CostEstimate(flops=0, bytes_accessed=1 << 16, transcendentals=0),
         name="prepare",
     )(*ints, bias, adj_one, adj_two, w_two, cot)
 
@@ -367,8 +384,10 @@
     down, adj_near, adj_far, weights, bias, table = call_prepare(
         plan, ints, bias_one.astype(jnp.float32).reshape(1, hidden), adj_one[0], adj_two[0], w_two, cotangent[0]
     )
-    near[1:], down = lax.optimization_barrier((near[1:], down))
-    far += [exchange(block, "feat", 1) for block in near[1:]]
+    near[1:-1], down = lax.optimization_barrier((near[1:-1], down))
+    far += [exchange(block, "feat", 1) for block in near[1:-1]]
+    near[-1], far[1:] = lax.optimization_barrier((near[-1], far[1:]))
+    far.append(exchange(near[-1], "feat", 1))
     gathered = [block for pair in zip(near, far) for block in pair]
     merge = max(1, 16 // feat_dev)
     if merge > 1:

time: 45.6 us -> 45 us (0.987)
  starting transfers between devices: 13.2 us -> 14.2 us
  Pallas kernels: 17.3 us -> 16.4 us
  waiting for transfers between devices: 10.9 us -> 10.3 us
    pallas_call x1, Pallas kernels: 7.52 us -> 6.23 us  [call_layer_one(): pl.pallas_call(functools.partial(layer_one_kernel, plan, blocks), out_sha...]
    ppermute x14, starting transfers between devices: 13.2 us -> 14.2 us  [exchange(): return lax.ppermute(array, axis, [(i, i ^ mask) for i in range(size)])]
    ppermute x14, waiting for transfers between devices: 10.9 us -> 10.3 us  [exchange(): return lax.ppermute(array, axis, [(i, i ^ mask) for i in range(size)])]
  transfers between devices with their start and end apart: 14 -> 14, of which waited for: 10 -> 8; matrix products, arithmetic and copies ran while one was open for 1% -> 1% of each run, Pallas kernels for 22% -> 23%
where the time goes in v3:
time: 45 us; the launch traced here: 44.6 us
  Pallas kernels  16.4 us (36%)
  starting transfers between devices  14.2 us (32%)
  waiting for transfers between devices  10.3 us (23%)
  other arithmetic  2.28 us (5%)
  local copies, waits for them, and re-layouts  0.73 us (2%)
  between operations  0.71 us (2%)
    ppermute x14, starting transfers between devices, exchange(): return lax.ppermute(array, axis, [(i, i ^ mask) for i in range(size)])  14.2 us
    ppermute x14, waiting for transfers between devices, exchange(): return lax.ppermute(array, axis, [(i, i ^ mask) for i in range(size)])  10.3 us
    pallas_call x1, Pallas kernels, call_prepare(): pl.pallas_call(functools.partial(prepare_kernel, plan), out_shape=(jax.Sh...  7.24 us
    pallas_call x1, Pallas kernels, call_layer_one(): pl.pallas_call(functools.partial(layer_one_kernel, plan, blocks), out_sha...  6.23 us
    pallas_call x1, Pallas kernels, call_layer_two(): pl.pallas_call(functools.partial(layer_two_kernel, plan), out_shape=jax.S...  2.93 us
    concatenate x1, other arithmetic, body(): packed = jnp.concatenate([x_local, w_one[0], w_one[1]], axis=1)  0.97 us
  transfers between devices with their start and end apart: 14, of which 8 were waited for; matrix products, arithmetic and copies ran while one was open for 1% of the time, Pallas kernels for 23%

profile of v3, /device:TPU:0, one launch (start us, length us, event | category | flops | bytes accessed | tf_op | source)
XLA Modules:
  0.0 44.6 jit_solution(17729129628936011006)
XLA Ops:
  0.6 0.7 %slice_bitcast_fusion.5 = (bf16[16,256]{1,0:T(8,128)(2,1)S(1)}, bf16[16,256]{1,0:T(8,128)(2,1)S(1)}) fusion(bf16[2,16,256]{2,1,0:T(8,128)(2,1)} %param.17), kind=kLoop, calls=%fused_computation.10 | loop fusion | bytes 32768 | tf_op jit(solution)/shard_map/squeeze | solution.py:379
  1.3 1.0 %pad_maximum_fusion.refs_0_ = bf16[16,8704]{1,0:T(8,128)(2,1)S(1)} fusion(bf16[16,256]{1,0:T(8,128)(2,1)S(1)} %get-tuple-element.36, bf16[16,256]{1,0:T(8,128)(2,1)S(1)} %get-tuple-element.35, bf16[16,8192]{1,0:T(8,128)(2,1)} %bitcast.33), kind=kLoop, calls=%fused_computation | loop fusion | flops 835584 | bytes 557056 | tf_op jit(solution)/shard_map/concatenate | solution.py:379
  2.3 3.0 %collective-permute-start.2 = (bf16[16,8704]{1,0:T(8,128)(2,1)S(1)}, bf16[16,8704]{1,0:T(8,128)(2,1)S(1)}, u32[]{:S(2)}, u32[]{:S(2)}) collective-permute-start(bf16[16,8704]{1,0:T(8,128)(2,1)S(1)} %pad_maximum_fusion.refs_0_), channel_id=1, source_target_pairs={{0,16},{4,20},{8,24},{12,28},{16,0},{20,4},{24,8},{28,12},{1,17},{... | collective-permute-start | bytes 835592 | tf_op jit(solution)/shard_map/ppermute | solution.py:25
  5.3 1.5 %collective-permute-start.1 = (bf16[16,8704]{1,0:T(8,128)(2,1)S(1)}, bf16[16,8704]{1,0:T(8,128)(2,1)S(1)}, u32[]{:S(2)}, u32[]{:S(2)}) collective-permute-start(bf16[16,8704]{1,0:T(8,128)(2,1)S(1)} %pad_maximum_fusion.refs_0_), channel_id=1, source_target_pairs={{0,8},{4,12},{8,0},{12,4},{16,24},{20,28},{24,16},{28,20},{1,9},{5... | collective-permute-start | bytes 835592 | tf_op jit(solution)/shard_map/ppermute | solution.py:25
  6.8 0.0 collective-permute-start.3
  6.9 0.7 %reshape.15 = f32[256]{0:T(256)S(1)} convert(bf16[256]{0:T(256)(128)(2,1)} %param.18) | non-fusion elementwise | flops 256 | bytes 1536 | tf_op jit(solution)/shard_map/reshape | solution.py:385
  7.5 7.2 %prepare.1 = (bf16[68,256,128]{2,1,0:T(8,128)(2,1)S(1)}, bf16[68,4,128,128]{3,2,1,0:T(8,128)(2,1)S(1)}, bf16[8,8,128,128]{3,2,1,0:T(8,128)(2,1)S(1)}, bf16[2,256...) custom-call(s32[1,64]{1,0:T(1,128)} %place_ref.1, s32[8,8]{1,0:T(8,128)} %bitcast.34, ...), custom_call_target="tpu_custom_call" | custom-call | bytes 65536 | tf_op jit(solution)/shard_map/prepare/pallas_call | solution.py:280
  14.8 0.0 collective-permute-done.2.refs_4_
  14.8 0.1 collective-permute-done.1.refs_2_
  14.9 0.0 collective-permute-start.4
  14.9 0.5 %collective-permute-start.5 = (bf16[16,8704]{1,0:T(8,128)(2,1)S(1)}, bf16[16,8704]{1,0:T(8,128)(2,1)S(1)}, u32[]{:S(2)}, u32[]{:S(2)}) collective-permute-start(bf16[16,8704]{1,0:T(8,128)(2,1)S(1)} %collective-permute-done.2.refs_4_), channel_id=1, source_target_pairs={{0,4},{4,0},{8,12},{12,8},{16,20},{20,16},{24,28},{28,24},{1,5},{5... | collective-permute-start | bytes 835592 | tf_op jit(solution)/shard_map/ppermute | solution.py:25
  15.4 0.0 collective-permute-start
  15.5 3.8 %collective-permute-done.3.refs_6_ = bf16[16,8704]{1,0:T(8,128)(2,1)S(1)} collective-permute-done((bf16[16,8704]{1,0:T(8,128)(2,1)S(1)}, bf16[16,8704]{1,0:T(8,128)(2,1)S(1)}, u32[]{:S(2)}, u32[]{:S(2)}) %collective-permute-start.3) | collective-permute-done | bytes 278560 | tf_op jit(solution)/shard_map/ppermute | solution.py:25
  19.2 0.0 collective-permute-done.4.refs_3_
  19.2 0.0 collective-permute-done.5.refs_5_
  19.2 0.0 collective-permute-start.6
  19.2 0.0 collective-permute-done.refs_1_
  19.3 1.5 %collective-permute-done.6.refs_7_ = bf16[16,8704]{1,0:T(8,128)(2,1)S(1)} collective-permute-done((bf16[16,8704]{1,0:T(8,128)(2,1)S(1)}, bf16[16,8704]{1,0:T(8,128)(2,1)S(1)}, u32[]{:S(2)}, u32[]{:S(2)}) %collective-permute-start.6) | collective-permute-done | bytes 278560 | tf_op jit(solution)/shard_map/ppermute | solution.py:25
  20.8 6.2 %layer_one.1 = (f32[4,2,16,256]{3,2,1,0:T(8,128)S(1)}, f32[4,2,16,256]{3,2,1,0:T(8,128)S(1)}, bf16[68,256,128]{2,1,0:T(8,128)(2,1)S(1)}) custom-call(s32[504]{0:T(512)S(1)} %get-tuple-element.17.table, bf16[16,8704]{1,0:T(8,128)(2,1)S(1)} %pad_maximum_fusion.refs_0_, bf16[16,8704]{1,0:T(8,128)(2,1)S(1)} %collective-permute-done.refs_1_, ...), custom_call_target="tpu_custom_call" | custom-call | flops 3221225472 | bytes 20971520 | tf_op jit(solution)/shard_map/layer_one/pallas_call | solution.py:314
  27.0 1.1 %collective-permute-start.7 = (f32[4,2,16,256]{3,2,1,0:T(8,128)S(1)}, f32[4,2,16,256]{3,2,1,0:T(8,128)S(1)}, u32[]{:S(2)}, u32[]{:S(2)}) collective-permute-start(f32[4,2,16,256]{3,2,1,0:T(8,128)S(1)} %get-tuple-element.31), channel_id=1, source_target_pairs={{0,4},{4,0},{8,12},{12,8},{16,20},{20,16},{24,28},{28,24},{1,5},{5... | collective-permute-start | bytes 393224 | tf_op jit(solution)/shard_map/ppermute | solution.py:25
  28.1 1.0 %collective-permute-done.7 = f32[4,2,16,256]{3,2,1,0:T(8,128)S(1)} collective-permute-done((f32[4,2,16,256]{3,2,1,0:T(8,128)S(1)}, f32[4,2,16,256]{3,2,1,0:T(8,128)S(1)}, u32[]{:S(2)}, u32[]{:S(2)}) %collective-permute-start.7) | collective-permute-done | bytes 131104 | tf_op jit(solution)/shard_map/ppermute | solution.py:25
  29.2 1.4 %collective-permute-start.8 = (f32[2,16,256]{2,1,0:T(8,128)S(1)}, f32[2,16,256]{2,1,0:T(8,128)S(1)}, u32[]{:S(2)}, u32[]{:S(2)}) collective-permute-start(f32[2,16,256]{2,1,0:T(8,128)S(1)} %get-tuple-element.32), channel_id=1, source_target_pairs={{0,8},{4,12},{8,0},{12,4},{16,24},{20,28},{24,16},{28,20},{1,9},{5... | collective-permute-start | bytes 98312 | tf_op jit(solution)/shard_map/ppermute | solution.py:25
  30.6 2.0 %collective-permute-start.10 = (f32[2,16,256]{2,1,0:T(8,128)S(1)}, f32[2,16,256]{2,1,0:T(8,128)S(1)}, u32[]{:S(2)}, u32[]{:S(2)}) collective-permute-start(f32[2,16,256]{2,1,0:T(8,128)S(1)} %get-tuple-element.33), channel_id=1, source_target_pairs={{0,24},{4,28},{8,16},{12,20},{16,8},{20,12},{24,0},{28,4},{1,25},{... | collective-permute-start | bytes 98312 | tf_op jit(solution)/shard_map/ppermute | solution.py:25
  32.6 0.2 collective-permute-start.9
  32.7 0.4 collective-permute-done.8
  33.2 2.3 %collective-permute-done.10 = f32[2,16,256]{2,1,0:T(8,128)S(1)} collective-permute-done((f32[2,16,256]{2,1,0:T(8,128)S(1)}, f32[2,16,256]{2,1,0:T(8,128)S(1)}, u32[]{:S(2)}, u32[]{:S(2)}) %collective-permute-start.10) | collective-permute-done | bytes 32800 | tf_op jit(solution)/shard_map/ppermute | solution.py:25
  35.5 1.0 %collective-permute-done.9 = f32[2,16,256]{2,1,0:T(8,128)S(1)} collective-permute-done((f32[2,16,256]{2,1,0:T(8,128)S(1)}, f32[2,16,256]{2,1,0:T(8,128)S(1)}, u32[]{:S(2)}, u32[]{:S(2)}) %collective-permute-start.9) | collective-permute-done | bytes 32800 | tf_op jit(solution)/shard_map/ppermute | solution.py:25
  36.5 2.5 %collective-permute-start.13 = (f32[2,16,256]{2,1,0:T(8,128)S(1)}, f32[2,16,256]{2,1,0:T(8,128)S(1)}, u32[]{:S(2)}, u32[]{:S(2)}) collective-permute-start(f32[2,16,256]{2,1,0:T(8,128)S(1)} %fusion.2), channel_id=1, source_target_pairs={{0,3},{1,2},{2,1},{3,0},{4,7},{5,6},{6,5},{7,4},{8,11},{9,10},{10,... | collective-permute-start | bytes 98312 | tf_op jit(solution)/shard_map/ppermute | solution.py:25
  39.0 0.0 collective-permute-start.12
  39.0 2.0 %collective-permute-start.11 = (f32[2,16,256]{2,1,0:T(8,128)S(1)}, f32[2,16,256]{2,1,0:T(8,128)S(1)}, u32[]{:S(2)}, u32[]{:S(2)}) collective-permute-start(f32[2,16,256]{2,1,0:T(8,128)S(1)} %fusion.2), channel_id=1, source_target_pairs={{0,1},{1,0},{2,3},{3,2},{4,5},{5,4},{6,7},{7,6},{8,9},{9,8},{10,11... | collective-permute-start | bytes 98312 | tf_op jit(solution)/shard_map/ppermute | solution.py:25
  41.0 2.9 %layer_two.1 = bf16[8,128,256]{2,1,0:T(8,128)(2,1)} custom-call(s32[504]{0:T(512)S(1)} %get-tuple-element.17.table, bf16[68,256,128]{2,1,0:T(8,128)(2,1)S(1)} %get-tuple-element.27.h_ref, bf16[8,8,128,128]{3,2,1,0:T(8,128)(2,1)S(1)} %get-tuple-element.28.adj_two, bf16[2,256,256]{2,1,0:T(8,128)(2,1)S(1)} %get-tuple-element.29.w_ref), custom_call_target="tpu_custom_call" | custom-call | flops 536870912 | bytes 8388608 | tf_op jit(solution)/shard_map/layer_two/pallas_call | solution.py:339
  43.9 0.0 collective-permute-done.13
  43.9 0.1 collective-permute-done.12
  44.0 0.0 collective-permute-done.11
  44.0 0.6 %add_add_fusion = f32[2,16,256]{2,1,0:T(8,128)} fusion(f32[2,16,256]{2,1,0:T(8,128)S(1)} %collective-permute-done.12, f32[2,16,256]{2,1,0:T(8,128)S(1)} %collective-permute-done.13, f32[2,16,256]{2,1,0:T(8,128)S(1)} %fusion.2, f32[2,16,256]{2,1,0:T(8,128)S(1)} %collective-permute-done.11), kind=kLoop, calls=%fused_computation.8 | loop fusion | flops 24576 | bytes 163840 | tf_op jit(solution)/shard_map/add | solution.py:406
  (3 shorter events, 0.0 us)
Async XLA Ops:
  2.3 12.5 %collective-permute-start.2 = (bf16[16,8704]{1,0:T(8,128)(2,1)S(1)}, bf16[16,8704]{1,0:T(8,128)(2,1)S(1)}, u32[]{:S(2)}, u32[]{:S(2)}) collective-permute-start(bf16[16,8704]{1,0:T(8,128)(2,1)S(1)} %pad_maximum_fusion.refs_0_), channel_id=1, source_target_pairs={{0,16},{4,20},{8,24},{12,28},{16,0},{20,4},{24,8},{28,12},{1,17},{... | collective-permute-start | bytes 835592 | tf_op jit(solution)/shard_map/ppermute | solution.py:25
  5.3 9.6 %collective-permute-start.1 = (bf16[16,8704]{1,0:T(8,128)(2,1)S(1)}, bf16[16,8704]{1,0:T(8,128)(2,1)S(1)}, u32[]{:S(2)}, u32[]{:S(2)}) collective-permute-start(bf16[16,8704]{1,0:T(8,128)(2,1)S(1)} %pad_maximum_fusion.refs_0_), channel_id=1, source_target_pairs={{0,8},{4,12},{8,0},{12,4},{16,24},{20,28},{24,16},{28,20},{1,9},{5... | collective-permute-start | bytes 835592 | tf_op jit(solution)/shard_map/ppermute | solution.py:25
  6.8 12.4 %collective-permute-start.3 = (bf16[16,8704]{1,0:T(8,128)(2,1)S(1)}, bf16[16,8704]{1,0:T(8,128)(2,1)S(1)}, u32[]{:S(2)}, u32[]{:S(2)}) collective-permute-start(bf16[16,8704]{1,0:T(8,128)(2,1)S(1)} %pad_maximum_fusion.refs_0_), channel_id=1, source_target_pairs={{0,24},{4,28},{8,16},{12,20},{16,8},{20,12},{24,0},{28,4},{1,25},{... | collective-permute-start | bytes 835592 | tf_op jit(solution)/shard_map/ppermute | solution.py:25
  14.9 4.3 %collective-permute-start.4 = (bf16[16,8704]{1,0:T(8,128)(2,1)S(1)}, bf16[16,8704]{1,0:T(8,128)(2,1)S(1)}, u32[]{:S(2)}, u32[]{:S(2)}) collective-permute-start(bf16[16,8704]{1,0:T(8,128)(2,1)S(1)} %collective-permute-done.1.refs_2_), channel_id=1, source_target_pairs={{0,4},{4,0},{8,12},{12,8},{16,20},{20,16},{24,28},{28,24},{1,5},{5... | collective-permute-start | bytes 835592 | tf_op jit(solution)/shard_map/ppermute | solution.py:25
  14.9 4.3 %collective-permute-start.5 = (bf16[16,8704]{1,0:T(8,128)(2,1)S(1)}, bf16[16,8704]{1,0:T(8,128)(2,1)S(1)}, u32[]{:S(2)}, u32[]{:S(2)}) collective-permute-start(bf16[16,8704]{1,0:T(8,128)(2,1)S(1)} %collective-permute-done.2.refs_4_), channel_id=1, source_target_pairs={{0,4},{4,0},{8,12},{12,8},{16,20},{20,16},{24,28},{28,24},{1,5},{5... | collective-permute-start | bytes 835592 | tf_op jit(solution)/shard_map/ppermute | solution.py:25
  15.4 3.8 %collective-permute-start = (bf16[16,8704]{1,0:T(8,128)(2,1)S(1)}, bf16[16,8704]{1,0:T(8,128)(2,1)S(1)}, u32[]{:S(2)}, u32[]{:S(2)}) collective-permute-start(bf16[16,8704]{1,0:T(8,128)(2,1)S(1)} %pad_maximum_fusion.refs_0_), channel_id=1, source_target_pairs={{0,4},{4,0},{8,12},{12,8},{16,20},{20,16},{24,28},{28,24},{1,5},{5... | collective-permute-start | bytes 835592 | tf_op jit(solution)/shard_map/ppermute | solution.py:25
  19.2 1.6 %collective-permute-start.6 = (bf16[16,8704]{1,0:T(8,128)(2,1)S(1)}, bf16[16,8704]{1,0:T(8,128)(2,1)S(1)}, u32[]{:S(2)}, u32[]{:S(2)}) collective-permute-start(bf16[16,8704]{1,0:T(8,128)(2,1)S(1)} %collective-permute-done.3.refs_6_), channel_id=1, source_target_pairs={{0,4},{4,0},{8,12},{12,8},{16,20},{20,16},{24,28},{28,24},{1,5},{5... | collective-permute-start | bytes 835592 | tf_op jit(solution)/shard_map/ppermute | solution.py:25
  27.0 2.1 %collective-permute-start.7 = (f32[4,2,16,256]{3,2,1,0:T(8,128)S(1)}, f32[4,2,16,256]{3,2,1,0:T(8,128)S(1)}, u32[]{:S(2)}, u32[]{:S(2)}) collective-permute-start(f32[4,2,16,256]{3,2,1,0:T(8,128)S(1)} %get-tuple-element.31), channel_id=1, source_target_pairs={{0,4},{4,0},{8,12},{12,8},{16,20},{20,16},{24,28},{28,24},{1,5},{5... | collective-permute-start | bytes 393224 | tf_op jit(solution)/shard_map/ppermute | solution.py:25
  29.2 4.0 %collective-permute-start.8 = (f32[2,16,256]{2,1,0:T(8,128)S(1)}, f32[2,16,256]{2,1,0:T(8,128)S(1)}, u32[]{:S(2)}, u32[]{:S(2)}) collective-permute-start(f32[2,16,256]{2,1,0:T(8,128)S(1)} %get-tuple-element.32), channel_id=1, source_target_pairs={{0,8},{4,12},{8,0},{12,4},{16,24},{20,28},{24,16},{28,20},{1,9},{5... | collective-permute-start | bytes 98312 | tf_op jit(solution)/shard_map/ppermute | solution.py:25
  30.6 4.9 %collective-permute-start.10 = (f32[2,16,256]{2,1,0:T(8,128)S(1)}, f32[2,16,256]{2,1,0:T(8,128)S(1)}, u32[]{:S(2)}, u32[]{:S(2)}) collective-permute-start(f32[2,16,256]{2,1,0:T(8,128)S(1)} %get-tuple-element.33), channel_id=1, source_target_pairs={{0,24},{4,28},{8,16},{12,20},{16,8},{20,12},{24,0},{28,4},{1,25},{... | collective-permute-start | bytes 98312 | tf_op jit(solution)/shard_map/ppermute | solution.py:25
  32.6 3.9 %collective-permute-start.9 = (f32[2,16,256]{2,1,0:T(8,128)S(1)}, f32[2,16,256]{2,1,0:T(8,128)S(1)}, u32[]{:S(2)}, u32[]{:S(2)}) collective-permute-start(f32[2,16,256]{2,1,0:T(8,128)S(1)} %get-tuple-element.34), channel_id=1, source_target_pairs={{0,16},{4,20},{8,24},{12,28},{16,0},{20,4},{24,8},{28,12},{1,17},{... | collective-permute-start | bytes 98312 | tf_op jit(solution)/shard_map/ppermute | solution.py:25
  36.5 7.4 %collective-permute-start.13 = (f32[2,16,256]{2,1,0:T(8,128)S(1)}, f32[2,16,256]{2,1,0:T(8,128)S(1)}, u32[]{:S(2)}, u32[]{:S(2)}) collective-permute-start(f32[2,16,256]{2,1,0:T(8,128)S(1)} %fusion.2), channel_id=1, source_target_pairs={{0,3},{1,2},{2,1},{3,0},{4,7},{5,6},{6,5},{7,4},{8,11},{9,10},{10,... | collective-permute-start | bytes 98312 | tf_op jit(solution)/shard_map/ppermute | solution.py:25
  39.0 5.0 %collective-permute-start.12 = (f32[2,16,256]{2,1,0:T(8,128)S(1)}, f32[2,16,256]{2,1,0:T(8,128)S(1)}, u32[]{:S(2)}, u32[]{:S(2)}) collective-permute-start(f32[2,16,256]{2,1,0:T(8,128)S(1)} %fusion.2), channel_id=1, source_target_pairs={{0,2},{1,3},{2,0},{3,1},{4,6},{5,7},{6,4},{7,5},{8,10},{9,11},{10,... | collective-permute-start | bytes 98312 | tf_op jit(solution)/shard_map/ppermute | solution.py:25
  39.0 5.0 %collective-permute-start.11 = (f32[2,16,256]{2,1,0:T(8,128)S(1)}, f32[2,16,256]{2,1,0:T(8,128)S(1)}, u32[]{:S(2)}, u32[]{:S(2)}) collective-permute-start(f32[2,16,256]{2,1,0:T(8,128)S(1)} %fusion.2), channel_id=1, source_target_pairs={{0,1},{1,0},{2,3},{3,2},{4,5},{5,4},{6,7},{7,6},{8,9},{9,8},{10,11... | collective-permute-start | bytes 98312 | tf_op jit(solution)/shard_map/ppermute | solution.py:25

commit v4 on v3

--- a/solution.py
+++ b/solution.py
@@ -32,7 +32,7 @@
         self.dense = self.entries == group_tiles
         self.slots = group_tiles if self.dense else self.entries + own
         self.few = fan_one // 2
-        self.steps = -(-self.slots // BATCH) + 1
+        self.steps = -(-self.slots // BATCH)
         self.padded = self.steps * BATCH
         self.tile_at = HEAD
         self.slot_at = self.tile_at + self.padded + BATCH
@@ -87,15 +87,6 @@
         if not plan.dense:
             active[plan.entries + p] = 1
 
-    def pad(start, end):
-        @pl.loop(start, end)
-        def _(i):
-            table[plan.tile_at + i] = 0
-            table[plan.slot_at + i] = plan.slots + lax.rem(i, BATCH)
-
-    def whole_steps(n):
-        return lax.div(n + BATCH - 1, BATCH)
-
     def visit(few, s, n):
         if plan.dense:
             placed = s
@@ -111,11 +102,15 @@
         return n + jnp.where(fits, active[s], 0)
 
     n = lax.fori_loop(0, plan.slots, functools.partial(visit, True), jnp.int32(0), unroll=8)
-    few_steps = whole_steps(n)
-    pad(n, few_steps * BATCH)
-    n = lax.fori_loop(0, plan.slots, functools.partial(visit, False), few_steps * BATCH, unroll=8)
-    steps = whole_steps(n)
-    pad(n, plan.padded + BATCH)
+    few_steps = lax.div(n, BATCH)
+    n = lax.fori_loop(0, plan.slots, functools.partial(visit, False), n, unroll=8)
+    steps = lax.div(n + BATCH - 1, BATCH)
+
+    @pl.loop(n, plan.padded + BATCH)
+    def _(i):
+        table[plan.tile_at + i] = 0
+        table[plan.slot_at + i] = plan.slots + lax.rem(i, BATCH)
+
     table[0] = steps
     table[1] = own_slot
     table[2] = few_steps

time: 45 us -> 45.2 us (level)
  starting transfers between devices: 14.2 us -> 13.3 us
  Pallas kernels: 16.4 us -> 16.9 us
    ppermute x14, starting transfers between devices: 14.2 us -> 13.3 us  [exchange(): return lax.ppermute(array, axis, [(i, i ^ mask) for i in range(size)])]
    ppermute x14, waiting for transfers between devices: 10.3 us -> 10.7 us  [exchange(): return lax.ppermute(array, axis, [(i, i ^ mask) for i in range(size)])]
  transfers between devices with their start and end apart: 14 -> 14, of which waited for: 8 -> 7; matrix products, arithmetic and copies ran while one was open for 1% -> 1% of each run, Pallas kernels for 23% -> 23%
where the time goes in v4:
time: 45.2 us; the launch traced here: 44.6 us
  Pallas kernels  16.9 us (37%)
  starting transfers between devices  13.3 us (29%)
  waiting for transfers between devices  10.7 us (24%)
  other arithmetic  2.28 us (5%)
  between operations  0.74 us (2%)
  local copies, waits for them, and re-layouts  0.73 us (2%)
    ppermute x14, starting transfers between devices, exchange(): return lax.ppermute(array, axis, [(i, i ^ mask) for i in range(size)])  13.3 us
    ppermute x14, waiting for transfers between devices, exchange(): return lax.ppermute(array, axis, [(i, i ^ mask) for i in range(size)])  10.7 us
    pallas_call x1, Pallas kernels, call_prepare(): pl.pallas_call(functools.partial(prepare_kernel, plan), out_shape=(jax.Sh...  7.39 us
    pallas_call x1, Pallas kernels, call_layer_one(): pl.pallas_call(functools.partial(layer_one_kernel, plan, blocks), out_sha...  6.55 us
    pallas_call x1, Pallas kernels, call_layer_two(): pl.pallas_call(functools.partial(layer_two_kernel, plan), out_shape=jax.S...  2.93 us
    concatenate x1, other arithmetic, body(): packed = jnp.concatenate([x_local, w_one[0], w_one[1]], axis=1)  0.97 us
  transfers between devices with their start and end apart: 14, of which 7 were waited for; matrix products, arithmetic and copies ran while one was open for 1% of the time, Pallas kernels for 23%

profile of v4, /device:TPU:0, one launch (start us, length us, event | category | flops | bytes accessed | tf_op | source)
XLA Modules:
  0.0 44.6 jit_solution(6418973227985327666)
XLA Ops:
  0.6 0.7 %slice_bitcast_fusion.5 = (bf16[16,256]{1,0:T(8,128)(2,1)S(1)}, bf16[16,256]{1,0:T(8,128)(2,1)S(1)}) fusion(bf16[2,16,256]{2,1,0:T(8,128)(2,1)} %param.17), kind=kLoop, calls=%fused_computation.10 | loop fusion | bytes 32768 | tf_op jit(solution)/shard_map/squeeze | solution.py:374
  1.3 1.0 %pad_maximum_fusion.refs_0_ = bf16[16,8704]{1,0:T(8,128)(2,1)S(1)} fusion(bf16[16,256]{1,0:T(8,128)(2,1)S(1)} %get-tuple-element.36, bf16[16,256]{1,0:T(8,128)(2,1)S(1)} %get-tuple-element.35, bf16[16,8192]{1,0:T(8,128)(2,1)} %bitcast.33), kind=kLoop, calls=%fused_computation | loop fusion | flops 835584 | bytes 557056 | tf_op jit(solution)/shard_map/concatenate | solution.py:374
  2.3 3.0 %collective-permute-start.2 = (bf16[16,8704]{1,0:T(8,128)(2,1)S(1)}, bf16[16,8704]{1,0:T(8,128)(2,1)S(1)}, u32[]{:S(2)}, u32[]{:S(2)}) collective-permute-start(bf16[16,8704]{1,0:T(8,128)(2,1)S(1)} %pad_maximum_fusion.refs_0_), channel_id=1, source_target_pairs={{0,16},{4,20},{8,24},{12,28},{16,0},{20,4},{24,8},{28,12},{1,17},{... | collective-permute-start | bytes 835592 | tf_op jit(solution)/shard_map/ppermute | solution.py:25
  5.3 1.5 %collective-permute-start.1 = (bf16[16,8704]{1,0:T(8,128)(2,1)S(1)}, bf16[16,8704]{1,0:T(8,128)(2,1)S(1)}, u32[]{:S(2)}, u32[]{:S(2)}) collective-permute-start(bf16[16,8704]{1,0:T(8,128)(2,1)S(1)} %pad_maximum_fusion.refs_0_), channel_id=1, source_target_pairs={{0,8},{4,12},{8,0},{12,4},{16,24},{20,28},{24,16},{28,20},{1,9},{5... | collective-permute-start | bytes 835592 | tf_op jit(solution)/shard_map/ppermute | solution.py:25
  6.8 0.0 collective-permute-start.3
  6.9 0.7 %reshape.15 = f32[256]{0:T(256)S(1)} convert(bf16[256]{0:T(256)(128)(2,1)} %param.18) | non-fusion elementwise | flops 256 | bytes 1536 | tf_op jit(solution)/shard_map/reshape | solution.py:380
  7.5 7.4 %prepare.1 = (bf16[68,256,128]{2,1,0:T(8,128)(2,1)S(1)}, bf16[64,4,128,128]{3,2,1,0:T(8,128)(2,1)S(1)}, bf16[8,8,128,128]{3,2,1,0:T(8,128)(2,1)S(1)}, bf16[2,256...) custom-call(s32[1,64]{1,0:T(1,128)} %place_ref.1, s32[8,8]{1,0:T(8,128)} %bitcast.34, ...), custom_call_target="tpu_custom_call" | custom-call | bytes 65536 | tf_op jit(solution)/shard_map/prepare/pallas_call | solution.py:275
  14.9 0.0 collective-permute-done.2.refs_4_
  15.0 0.0 collective-permute-done.1.refs_2_
  15.0 0.1 collective-permute-start.4
  15.1 0.5 %collective-permute-start.5 = (bf16[16,8704]{1,0:T(8,128)(2,1)S(1)}, bf16[16,8704]{1,0:T(8,128)(2,1)S(1)}, u32[]{:S(2)}, u32[]{:S(2)}) collective-permute-start(bf16[16,8704]{1,0:T(8,128)(2,1)S(1)} %collective-permute-done.2.refs_4_), channel_id=1, source_target_pairs={{0,4},{4,0},{8,12},{12,8},{16,20},{20,16},{24,28},{28,24},{1,5},{5... | collective-permute-start | bytes 835592 | tf_op jit(solution)/shard_map/ppermute | solution.py:25
  15.5 0.1 collective-permute-start
  15.6 3.6 %collective-permute-done.3.refs_6_ = bf16[16,8704]{1,0:T(8,128)(2,1)S(1)} collective-permute-done((bf16[16,8704]{1,0:T(8,128)(2,1)S(1)}, bf16[16,8704]{1,0:T(8,128)(2,1)S(1)}, u32[]{:S(2)}, u32[]{:S(2)}) %collective-permute-start.3) | collective-permute-done | bytes 278560 | tf_op jit(solution)/shard_map/ppermute | solution.py:25
  19.2 0.0 collective-permute-done.4.refs_3_
  19.2 0.0 collective-permute-done.5.refs_5_
  19.2 0.0 collective-permute-start.6
  19.2 0.0 collective-permute-done.refs_1_
  19.3 1.5 %collective-permute-done.6.refs_7_ = bf16[16,8704]{1,0:T(8,128)(2,1)S(1)} collective-permute-done((bf16[16,8704]{1,0:T(8,128)(2,1)S(1)}, bf16[16,8704]{1,0:T(8,128)(2,1)S(1)}, u32[]{:S(2)}, u32[]{:S(2)}) %collective-permute-start.6) | collective-permute-done | bytes 278560 | tf_op jit(solution)/shard_map/ppermute | solution.py:25
  20.8 6.5 %layer_one.1 = (f32[4,2,16,256]{3,2,1,0:T(8,128)S(1)}, f32[4,2,16,256]{3,2,1,0:T(8,128)S(1)}, bf16[68,256,128]{2,1,0:T(8,128)(2,1)S(1)}) custom-call(s32[480]{0:T(512)S(1)} %get-tuple-element.17.table, bf16[16,8704]{1,0:T(8,128)(2,1)S(1)} %pad_maximum_fusion.refs_0_, bf16[16,8704]{1,0:T(8,128)(2,1)S(1)} %collective-permute-done.refs_1_, ...), custom_call_target="tpu_custom_call" | custom-call | flops 3221225472 | bytes 20971520 | tf_op jit(solution)/shard_map/layer_one/pallas_call | solution.py:309
  27.4 0.1 collective-permute-start.7
  27.4 1.3 %collective-permute-done.7 = f32[4,2,16,256]{3,2,1,0:T(8,128)S(1)} collective-permute-done((f32[4,2,16,256]{3,2,1,0:T(8,128)S(1)}, f32[4,2,16,256]{3,2,1,0:T(8,128)S(1)}, u32[]{:S(2)}, u32[]{:S(2)}) %collective-permute-start.7) | collective-permute-done | bytes 131104 | tf_op jit(solution)/shard_map/ppermute | solution.py:25
  28.8 1.8 %collective-permute-start.8 = (f32[2,16,256]{2,1,0:T(8,128)S(1)}, f32[2,16,256]{2,1,0:T(8,128)S(1)}, u32[]{:S(2)}, u32[]{:S(2)}) collective-permute-start(f32[2,16,256]{2,1,0:T(8,128)S(1)} %get-tuple-element.32), channel_id=1, source_target_pairs={{0,8},{4,12},{8,0},{12,4},{16,24},{20,28},{24,16},{28,20},{1,9},{5... | collective-permute-start | bytes 98312 | tf_op jit(solution)/shard_map/ppermute | solution.py:25
  30.6 1.1 %collective-permute-start.10 = (f32[2,16,256]{2,1,0:T(8,128)S(1)}, f32[2,16,256]{2,1,0:T(8,128)S(1)}, u32[]{:S(2)}, u32[]{:S(2)}) collective-permute-start(f32[2,16,256]{2,1,0:T(8,128)S(1)} %get-tuple-element.33), channel_id=1, source_target_pairs={{0,24},{4,28},{8,16},{12,20},{16,8},{20,12},{24,0},{28,4},{1,25},{... | collective-permute-start | bytes 98312 | tf_op jit(solution)/shard_map/ppermute | solution.py:25
  31.7 0.7 %collective-permute-start.9 = (f32[2,16,256]{2,1,0:T(8,128)S(1)}, f32[2,16,256]{2,1,0:T(8,128)S(1)}, u32[]{:S(2)}, u32[]{:S(2)}) collective-permute-start(f32[2,16,256]{2,1,0:T(8,128)S(1)} %get-tuple-element.34), channel_id=1, source_target_pairs={{0,16},{4,20},{8,24},{12,28},{16,0},{20,4},{24,8},{28,12},{1,17},{... | collective-permute-start | bytes 98312 | tf_op jit(solution)/shard_map/ppermute | solution.py:25
  32.4 0.4 collective-permute-done.8
  32.8 2.6 %collective-permute-done.10 = f32[2,16,256]{2,1,0:T(8,128)S(1)} collective-permute-done((f32[2,16,256]{2,1,0:T(8,128)S(1)}, f32[2,16,256]{2,1,0:T(8,128)S(1)}, u32[]{:S(2)}, u32[]{:S(2)}) %collective-permute-start.10) | collective-permute-done | bytes 32800 | tf_op jit(solution)/shard_map/ppermute | solution.py:25
  35.4 0.3 collective-permute-done.9
  35.8 3.4 %collective-permute-start.13 = (f32[2,16,256]{2,1,0:T(8,128)S(1)}, f32[2,16,256]{2,1,0:T(8,128)S(1)}, u32[]{:S(2)}, u32[]{:S(2)}) collective-permute-start(f32[2,16,256]{2,1,0:T(8,128)S(1)} %fusion.2), channel_id=1, source_target_pairs={{0,3},{1,2},{2,1},{3,0},{4,7},{5,6},{6,5},{7,4},{8,11},{9,10},{10,... | collective-permute-start | bytes 98312 | tf_op jit(solution)/shard_map/ppermute | solution.py:25
  39.2 0.0 collective-permute-start.12
  39.2 1.0 %collective-permute-start.11 = (f32[2,16,256]{2,1,0:T(8,128)S(1)}, f32[2,16,256]{2,1,0:T(8,128)S(1)}, u32[]{:S(2)}, u32[]{:S(2)}) collective-permute-start(f32[2,16,256]{2,1,0:T(8,128)S(1)} %fusion.2), channel_id=1, source_target_pairs={{0,1},{1,0},{2,3},{3,2},{4,5},{5,4},{6,7},{7,6},{8,9},{9,8},{10,11... | collective-permute-start | bytes 98312 | tf_op jit(solution)/shard_map/ppermute | solution.py:25
  40.2 2.9 %layer_two.1 = bf16[8,128,256]{2,1,0:T(8,128)(2,1)} custom-call(s32[480]{0:T(512)S(1)} %get-tuple-element.17.table, bf16[68,256,128]{2,1,0:T(8,128)(2,1)S(1)} %get-tuple-element.27.h_ref, bf16[8,8,128,128]{3,2,1,0:T(8,128)(2,1)S(1)} %get-tuple-element.28.adj_two, bf16[2,256,256]{2,1,0:T(8,128)(2,1)S(1)} %get-tuple-element.29.w_ref), custom_call_target="tpu_custom_call" | custom-call | flops 536870912 | bytes 8388608 | tf_op jit(solution)/shard_map/layer_two/pallas_call | solution.py:334
  43.2 0.0 collective-permute-done.13
  43.2 0.8 %collective-permute-done.12 = f32[2,16,256]{2,1,0:T(8,128)S(1)} collective-permute-done((f32[2,16,256]{2,1,0:T(8,128)S(1)}, f32[2,16,256]{2,1,0:T(8,128)S(1)}, u32[]{:S(2)}, u32[]{:S(2)}) %collective-permute-start.12) | collective-permute-done | bytes 32800 | tf_op jit(solution)/shard_map/ppermute | solution.py:25
  44.0 0.0 collective-permute-done.11
  44.0 0.6 %add_add_fusion = f32[2,16,256]{2,1,0:T(8,128)} fusion(f32[2,16,256]{2,1,0:T(8,128)S(1)} %collective-permute-done.12, f32[2,16,256]{2,1,0:T(8,128)S(1)} %collective-permute-done.13, f32[2,16,256]{2,1,0:T(8,128)S(1)} %fusion.2, f32[2,16,256]{2,1,0:T(8,128)S(1)} %collective-permute-done.11), kind=kLoop, calls=%fused_computation.8 | loop fusion | flops 24576 | bytes 163840 | tf_op jit(solution)/shard_map/add | solution.py:401
  (3 shorter events, 0.0 us)
Async XLA Ops:
  2.3 12.6 %collective-permute-start.2 = (bf16[16,8704]{1,0:T(8,128)(2,1)S(1)}, bf16[16,8704]{1,0:T(8,128)(2,1)S(1)}, u32[]{:S(2)}, u32[]{:S(2)}) collective-permute-start(bf16[16,8704]{1,0:T(8,128)(2,1)S(1)} %pad_maximum_fusion.refs_0_), channel_id=1, source_target_pairs={{0,16},{4,20},{8,24},{12,28},{16,0},{20,4},{24,8},{28,12},{1,17},{... | collective-permute-start | bytes 835592 | tf_op jit(solution)/shard_map/ppermute | solution.py:25
  5.3 9.6 %collective-permute-start.1 = (bf16[16,8704]{1,0:T(8,128)(2,1)S(1)}, bf16[16,8704]{1,0:T(8,128)(2,1)S(1)}, u32[]{:S(2)}, u32[]{:S(2)}) collective-permute-start(bf16[16,8704]{1,0:T(8,128)(2,1)S(1)} %pad_maximum_fusion.refs_0_), channel_id=1, source_target_pairs={{0,8},{4,12},{8,0},{12,4},{16,24},{20,28},{24,16},{28,20},{1,9},{5... | collective-permute-start | bytes 835592 | tf_op jit(solution)/shard_map/ppermute | solution.py:25
  6.8 12.4 %collective-permute-start.3 = (bf16[16,8704]{1,0:T(8,128)(2,1)S(1)}, bf16[16,8704]{1,0:T(8,128)(2,1)S(1)}, u32[]{:S(2)}, u32[]{:S(2)}) collective-permute-start(bf16[16,8704]{1,0:T(8,128)(2,1)S(1)} %pad_maximum_fusion.refs_0_), channel_id=1, source_target_pairs={{0,24},{4,28},{8,16},{12,20},{16,8},{20,12},{24,0},{28,4},{1,25},{... | collective-permute-start | bytes 835592 | tf_op jit(solution)/shard_map/ppermute | solution.py:25
  15.0 4.3 %collective-permute-start.4 = (bf16[16,8704]{1,0:T(8,128)(2,1)S(1)}, bf16[16,8704]{1,0:T(8,128)(2,1)S(1)}, u32[]{:S(2)}, u32[]{:S(2)}) collective-permute-start(bf16[16,8704]{1,0:T(8,128)(2,1)S(1)} %collective-permute-done.1.refs_2_), channel_id=1, source_target_pairs={{0,4},{4,0},{8,12},{12,8},{16,20},{20,16},{24,28},{28,24},{1,5},{5... | collective-permute-start | bytes 835592 | tf_op jit(solution)/shard_map/ppermute | solution.py:25
  15.1 4.2 %collective-permute-start.5 = (bf16[16,8704]{1,0:T(8,128)(2,1)S(1)}, bf16[16,8704]{1,0:T(8,128)(2,1)S(1)}, u32[]{:S(2)}, u32[]{:S(2)}) collective-permute-start(bf16[16,8704]{1,0:T(8,128)(2,1)S(1)} %collective-permute-done.2.refs_4_), channel_id=1, source_target_pairs={{0,4},{4,0},{8,12},{12,8},{16,20},{20,16},{24,28},{28,24},{1,5},{5... | collective-permute-start | bytes 835592 | tf_op jit(solution)/shard_map/ppermute | solution.py:25
  15.5 3.7 %collective-permute-start = (bf16[16,8704]{1,0:T(8,128)(2,1)S(1)}, bf16[16,8704]{1,0:T(8,128)(2,1)S(1)}, u32[]{:S(2)}, u32[]{:S(2)}) collective-permute-start(bf16[16,8704]{1,0:T(8,128)(2,1)S(1)} %pad_maximum_fusion.refs_0_), channel_id=1, source_target_pairs={{0,4},{4,0},{8,12},{12,8},{16,20},{20,16},{24,28},{28,24},{1,5},{5... | collective-permute-start | bytes 835592 | tf_op jit(solution)/shard_map/ppermute | solution.py:25
  19.2 1.6 %collective-permute-start.6 = (bf16[16,8704]{1,0:T(8,128)(2,1)S(1)}, bf16[16,8704]{1,0:T(8,128)(2,1)S(1)}, u32[]{:S(2)}, u32[]{:S(2)}) collective-permute-start(bf16[16,8704]{1,0:T(8,128)(2,1)S(1)} %collective-permute-done.3.refs_6_), channel_id=1, source_target_pairs={{0,4},{4,0},{8,12},{12,8},{16,20},{20,16},{24,28},{28,24},{1,5},{5... | collective-permute-start | bytes 835592 | tf_op jit(solution)/shard_map/ppermute | solution.py:25
  27.4 1.4 %collective-permute-start.7 = (f32[4,2,16,256]{3,2,1,0:T(8,128)S(1)}, f32[4,2,16,256]{3,2,1,0:T(8,128)S(1)}, u32[]{:S(2)}, u32[]{:S(2)}) collective-permute-start(f32[4,2,16,256]{3,2,1,0:T(8,128)S(1)} %get-tuple-element.31), channel_id=1, source_target_pairs={{0,4},{4,0},{8,12},{12,8},{16,20},{20,16},{24,28},{28,24},{1,5},{5... | collective-permute-start | bytes 393224 | tf_op jit(solution)/shard_map/ppermute | solution.py:25
  28.8 4.0 %collective-permute-start.8 = (f32[2,16,256]{2,1,0:T(8,128)S(1)}, f32[2,16,256]{2,1,0:T(8,128)S(1)}, u32[]{:S(2)}, u32[]{:S(2)}) collective-permute-start(f32[2,16,256]{2,1,0:T(8,128)S(1)} %get-tuple-element.32), channel_id=1, source_target_pairs={{0,8},{4,12},{8,0},{12,4},{16,24},{20,28},{24,16},{28,20},{1,9},{5... | collective-permute-start | bytes 98312 | tf_op jit(solution)/shard_map/ppermute | solution.py:25
  30.6 4.8 %collective-permute-start.10 = (f32[2,16,256]{2,1,0:T(8,128)S(1)}, f32[2,16,256]{2,1,0:T(8,128)S(1)}, u32[]{:S(2)}, u32[]{:S(2)}) collective-permute-start(f32[2,16,256]{2,1,0:T(8,128)S(1)} %get-tuple-element.33), channel_id=1, source_target_pairs={{0,24},{4,28},{8,16},{12,20},{16,8},{20,12},{24,0},{28,4},{1,25},{... | collective-permute-start | bytes 98312 | tf_op jit(solution)/shard_map/ppermute | solution.py:25
  31.7 4.1 %collective-permute-start.9 = (f32[2,16,256]{2,1,0:T(8,128)S(1)}, f32[2,16,256]{2,1,0:T(8,128)S(1)}, u32[]{:S(2)}, u32[]{:S(2)}) collective-permute-start(f32[2,16,256]{2,1,0:T(8,128)S(1)} %get-tuple-element.34), channel_id=1, source_target_pairs={{0,16},{4,20},{8,24},{12,28},{16,0},{20,4},{24,8},{28,12},{1,17},{... | collective-permute-start | bytes 98312 | tf_op jit(solution)/shard_map/ppermute | solution.py:25
  35.8 7.4 %collective-permute-start.13 = (f32[2,16,256]{2,1,0:T(8,128)S(1)}, f32[2,16,256]{2,1,0:T(8,128)S(1)}, u32[]{:S(2)}, u32[]{:S(2)}) collective-permute-start(f32[2,16,256]{2,1,0:T(8,128)S(1)} %fusion.2), channel_id=1, source_target_pairs={{0,3},{1,2},{2,1},{3,0},{4,7},{5,6},{6,5},{7,4},{8,11},{9,10},{10,... | collective-permute-start | bytes 98312 | tf_op jit(solution)/shard_map/ppermute | solution.py:25
  39.2 4.8 %collective-permute-start.12 = (f32[2,16,256]{2,1,0:T(8,128)S(1)}, f32[2,16,256]{2,1,0:T(8,128)S(1)}, u32[]{:S(2)}, u32[]{:S(2)}) collective-permute-start(f32[2,16,256]{2,1,0:T(8,128)S(1)} %fusion.2), channel_id=1, source_target_pairs={{0,2},{1,3},{2,0},{3,1},{4,6},{5,7},{6,4},{7,5},{8,10},{9,11},{10,... | collective-permute-start | bytes 98312 | tf_op jit(solution)/shard_map/ppermute | solution.py:25
  39.2 4.8 %collective-permute-start.11 = (f32[2,16,256]{2,1,0:T(8,128)S(1)}, f32[2,16,256]{2,1,0:T(8,128)S(1)}, u32[]{:S(2)}, u32[]{:S(2)}) collective-permute-start(f32[2,16,256]{2,1,0:T(8,128)S(1)} %fusion.2), channel_id=1, source_target_pairs={{0,1},{1,0},{2,3},{3,2},{4,5},{5,4},{6,7},{7,6},{8,9},{9,8},{10,11... | collective-permute-start | bytes 98312 | tf_op jit(solution)/shard_map/ppermute | solution.py:25

commit v5 on v4

--- a/solution.py
+++ b/solution.py
@@ -243,7 +243,7 @@
         out = even_ref if m % 2 == 0 else odd_ref
         for part in range(2):
             at = part * features + m * share
-            out[m // 2, part] = 0.5 * total[at : at + share]
+            out[m // 2, part] = (0.5 * total[at : at + share]).astype(out.dtype)
 
 
 def layer_two_kernel(plan, table, h_ref, adj_two, w_ref, out_ref, agg, out, sems):
@@ -308,7 +308,7 @@
     share = jax.ShapeDtypeStruct((feat_count // 2, 2, features // feat_count, hidden), jnp.float32)
     return pl.pallas_call(
         functools.partial(layer_one_kernel, plan, blocks),
-        out_shape=(share, share, jax.ShapeDtypeStruct(down.shape, kind)),
+        out_shape=(share, jax.ShapeDtypeStruct(share.shape, kind), jax.ShapeDtypeStruct(down.shape, kind)),
         in_specs=[SMEM] + [VMEM] * (blocks + 3),
         out_specs=(VMEM,) * 3,
         scratch_shapes=[
@@ -392,7 +392,7 @@
     even, odd, h_tiles = call_layer_one(plan, feat_count, table, gathered, bias, adj_near, down)
     layer_out = call_layer_two(plan, table, h_tiles, adj_far, weights)
 
-    even = even + exchange(odd, "feat", 1)
+    even = even + exchange(odd, "feat", 1).astype(jnp.float32)
     grad = even[0]
     for received in [exchange(even[j], "feat", 2 * j) for j in range(1, feat_count // 2)]:
         grad = grad + received

time: 45.2 us -> 45 us (level)
  Pallas kernels: 16.9 us -> 16.3 us
  transfers between devices with their start and end apart: 14 -> 14, of which waited for: 7 -> 8; matrix products, arithmetic and copies ran while one was open for 1% -> 1% of each run, Pallas kernels for 23% -> 23%
where the time goes in v5:
time: 45 us; the launch traced here: 44.4 us
  Pallas kernels  16.3 us (36%)
  starting transfers between devices  13.3 us (30%)
  waiting for transfers between devices  11 us (24%)
  other arithmetic  2.28 us (5%)
  local copies, waits for them, and re-layouts  0.73 us (2%)
  between operations  0.71 us (2%)
    ppermute x14, starting transfers between devices, exchange(): return lax.ppermute(array, axis, [(i, i ^ mask) for i in range(size)])  13.3 us
    ppermute x14, waiting for transfers between devices, exchange(): return lax.ppermute(array, axis, [(i, i ^ mask) for i in range(size)])  11 us
    pallas_call x1, Pallas kernels, call_prepare(): pl.pallas_call(functools.partial(prepare_kernel, plan), out_shape=(jax.Sh...  7.09 us
    pallas_call x1, Pallas kernels, call_layer_one(): pl.pallas_call(functools.partial(layer_one_kernel, plan, blocks), out_sha...  6.31 us
    pallas_call x1, Pallas kernels, call_layer_two(): pl.pallas_call(functools.partial(layer_two_kernel, plan), out_shape=jax.S...  2.93 us
    concatenate x1, other arithmetic, body(): packed = jnp.concatenate([x_local, w_one[0], w_one[1]], axis=1)  0.97 us
  transfers between devices with their start and end apart: 14, of which 8 were waited for; matrix products, arithmetic and copies ran while one was open for 1% of the time, Pallas kernels for 23%

profile of v5, /device:TPU:0, one launch (start us, length us, event | category | flops | bytes accessed | tf_op | source)
XLA Modules:
  0.0 44.4 jit_solution(14356970339386801024)
XLA Ops:
  0.6 0.7 %slice_bitcast_fusion.5 = (bf16[16,256]{1,0:T(8,128)(2,1)S(1)}, bf16[16,256]{1,0:T(8,128)(2,1)S(1)}) fusion(bf16[2,16,256]{2,1,0:T(8,128)(2,1)} %param.17), kind=kLoop, calls=%fused_computation.11 | loop fusion | bytes 32768 | tf_op jit(solution)/shard_map/squeeze | solution.py:374
  1.3 1.0 %pad_maximum_fusion.refs_0_ = bf16[16,8704]{1,0:T(8,128)(2,1)S(1)} fusion(bf16[16,256]{1,0:T(8,128)(2,1)S(1)} %get-tuple-element.36, bf16[16,256]{1,0:T(8,128)(2,1)S(1)} %get-tuple-element.35, bf16[16,8192]{1,0:T(8,128)(2,1)} %bitcast.33), kind=kLoop, calls=%fused_computation | loop fusion | flops 835584 | bytes 557056 | tf_op jit(solution)/shard_map/concatenate | solution.py:374
  2.3 3.0 %collective-permute-start.2 = (bf16[16,8704]{1,0:T(8,128)(2,1)S(1)}, bf16[16,8704]{1,0:T(8,128)(2,1)S(1)}, u32[]{:S(2)}, u32[]{:S(2)}) collective-permute-start(bf16[16,8704]{1,0:T(8,128)(2,1)S(1)} %pad_maximum_fusion.refs_0_), channel_id=1, source_target_pairs={{0,16},{4,20},{8,24},{12,28},{16,0},{20,4},{24,8},{28,12},{1,17},{... | collective-permute-start | bytes 835592 | tf_op jit(solution)/shard_map/ppermute | solution.py:25
  5.3 1.5 %collective-permute-start.1 = (bf16[16,8704]{1,0:T(8,128)(2,1)S(1)}, bf16[16,8704]{1,0:T(8,128)(2,1)S(1)}, u32[]{:S(2)}, u32[]{:S(2)}) collective-permute-start(bf16[16,8704]{1,0:T(8,128)(2,1)S(1)} %pad_maximum_fusion.refs_0_), channel_id=1, source_target_pairs={{0,8},{4,12},{8,0},{12,4},{16,24},{20,28},{24,16},{28,20},{1,9},{5... | collective-permute-start | bytes 835592 | tf_op jit(solution)/shard_map/ppermute | solution.py:25
  6.8 0.0 collective-permute-start.3
  6.9 0.7 %reshape.15 = f32[256]{0:T(256)S(1)} convert(bf16[256]{0:T(256)(128)(2,1)} %param.18) | non-fusion elementwise | flops 256 | bytes 1536 | tf_op jit(solution)/shard_map/reshape | solution.py:380
  7.5 7.1 %prepare.1 = (bf16[68,256,128]{2,1,0:T(8,128)(2,1)S(1)}, bf16[64,4,128,128]{3,2,1,0:T(8,128)(2,1)S(1)}, bf16[8,8,128,128]{3,2,1,0:T(8,128)(2,1)S(1)}, bf16[2,256...) custom-call(s32[1,64]{1,0:T(1,128)} %place_ref.1, s32[8,8]{1,0:T(8,128)} %bitcast.34, ...), custom_call_target="tpu_custom_call" | custom-call | bytes 65536 | tf_op jit(solution)/shard_map/prepare/pallas_call | solution.py:275
  14.6 0.0 collective-permute-done.2.refs_4_
  14.7 0.3 collective-permute-done.1.refs_2_
  14.9 0.0 collective-permute-start.4
  14.9 0.5 %collective-permute-start.5 = (bf16[16,8704]{1,0:T(8,128)(2,1)S(1)}, bf16[16,8704]{1,0:T(8,128)(2,1)S(1)}, u32[]{:S(2)}, u32[]{:S(2)}) collective-permute-start(bf16[16,8704]{1,0:T(8,128)(2,1)S(1)} %collective-permute-done.2.refs_4_), channel_id=1, source_target_pairs={{0,4},{4,0},{8,12},{12,8},{16,20},{20,16},{24,28},{28,24},{1,5},{5... | collective-permute-start | bytes 835592 | tf_op jit(solution)/shard_map/ppermute | solution.py:25
  15.4 0.0 collective-permute-start
  15.4 3.8 %collective-permute-done.3.refs_6_ = bf16[16,8704]{1,0:T(8,128)(2,1)S(1)} collective-permute-done((bf16[16,8704]{1,0:T(8,128)(2,1)S(1)}, bf16[16,8704]{1,0:T(8,128)(2,1)S(1)}, u32[]{:S(2)}, u32[]{:S(2)}) %collective-permute-start.3) | collective-permute-done | bytes 278560 | tf_op jit(solution)/shard_map/ppermute | solution.py:25
  19.2 0.0 collective-permute-done.4.refs_3_
  19.2 0.0 collective-permute-done.5.refs_5_
  19.2 0.0 collective-permute-start.6
  19.2 0.0 collective-permute-done.refs_1_
  19.3 1.5 %collective-permute-done.6.refs_7_ = bf16[16,8704]{1,0:T(8,128)(2,1)S(1)} collective-permute-done((bf16[16,8704]{1,0:T(8,128)(2,1)S(1)}, bf16[16,8704]{1,0:T(8,128)(2,1)S(1)}, u32[]{:S(2)}, u32[]{:S(2)}) %collective-permute-start.6) | collective-permute-done | bytes 278560 | tf_op jit(solution)/shard_map/ppermute | solution.py:25
  20.8 6.3 %layer_one.1 = (f32[4,2,16,256]{3,2,1,0:T(8,128)S(1)}, bf16[4,2,16,256]{3,2,1,0:T(8,128)(2,1)S(1)}, bf16[68,256,128]{2,1,0:T(8,128)(2,1)S(1)}) custom-call(s32[480]{0:T(512)S(1)} %get-tuple-element.17.table, bf16[16,8704]{1,0:T(8,128)(2,1)S(1)} %pad_maximum_fusion.refs_0_, bf16[16,8704]{1,0:T(8,128)(2,1)S(1)} %collective-permute-done.refs_1_, ...), custom_call_target="tpu_custom_call" | custom-call | flops 3221225472 | bytes 20971520 | tf_op jit(solution)/shard_map/layer_one/pallas_call | solution.py:309
  27.1 0.2 collective-permute-start.7
  27.3 1.1 %collective-permute-done.7 = bf16[4,2,16,256]{3,2,1,0:T(8,128)(2,1)S(1)} collective-permute-done((bf16[4,2,16,256]{3,2,1,0:T(8,128)(2,1)S(1)}, bf16[4,2,16,256]{3,2,1,0:T(8,128)(2,1)S(1)}, u32[]{:S(2)}, u32[]{:S(2)}) %collective-permute-start.7) | collective-permute-done | bytes 65568 | tf_op jit(solution)/shard_map/ppermute | solution.py:25
  28.5 1.5 %collective-permute-start.8 = (f32[2,16,256]{2,1,0:T(8,128)S(1)}, f32[2,16,256]{2,1,0:T(8,128)S(1)}, u32[]{:S(2)}, u32[]{:S(2)}) collective-permute-start(f32[2,16,256]{2,1,0:T(8,128)S(1)} %get-tuple-element.32), channel_id=1, source_target_pairs={{0,8},{4,12},{8,0},{12,4},{16,24},{20,28},{24,16},{28,20},{1,9},{5... | collective-permute-start | bytes 98312 | tf_op jit(solution)/shard_map/ppermute | solution.py:25
  30.0 2.0 %collective-permute-start.10 = (f32[2,16,256]{2,1,0:T(8,128)S(1)}, f32[2,16,256]{2,1,0:T(8,128)S(1)}, u32[]{:S(2)}, u32[]{:S(2)}) collective-permute-start(f32[2,16,256]{2,1,0:T(8,128)S(1)} %get-tuple-element.33), channel_id=1, source_target_pairs={{0,24},{4,28},{8,16},{12,20},{16,8},{20,12},{24,0},{28,4},{1,25},{... | collective-permute-start | bytes 98312 | tf_op jit(solution)/shard_map/ppermute | solution.py:25
  31.9 0.1 collective-permute-start.9
  32.0 0.4 collective-permute-done.8
  32.5 2.4 %collective-permute-done.10 = f32[2,16,256]{2,1,0:T(8,128)S(1)} collective-permute-done((f32[2,16,256]{2,1,0:T(8,128)S(1)}, f32[2,16,256]{2,1,0:T(8,128)S(1)}, u32[]{:S(2)}, u32[]{:S(2)}) %collective-permute-start.10) | collective-permute-done | bytes 32800 | tf_op jit(solution)/shard_map/ppermute | solution.py:25
  34.9 1.0 %collective-permute-done.9 = f32[2,16,256]{2,1,0:T(8,128)S(1)} collective-permute-done((f32[2,16,256]{2,1,0:T(8,128)S(1)}, f32[2,16,256]{2,1,0:T(8,128)S(1)}, u32[]{:S(2)}, u32[]{:S(2)}) %collective-permute-start.9) | collective-permute-done | bytes 32800 | tf_op jit(solution)/shard_map/ppermute | solution.py:25
  35.9 3.1 %collective-permute-start.13 = (f32[2,16,256]{2,1,0:T(8,128)S(1)}, f32[2,16,256]{2,1,0:T(8,128)S(1)}, u32[]{:S(2)}, u32[]{:S(2)}) collective-permute-start(f32[2,16,256]{2,1,0:T(8,128)S(1)} %fusion.2), channel_id=1, source_target_pairs={{0,3},{1,2},{2,1},{3,0},{4,7},{5,6},{6,5},{7,4},{8,11},{9,10},{10,... | collective-permute-start | bytes 98312 | tf_op jit(solution)/shard_map/ppermute | solution.py:25
  38.9 0.0 collective-permute-start.12
  38.9 1.4 %collective-permute-start.11 = (f32[2,16,256]{2,1,0:T(8,128)S(1)}, f32[2,16,256]{2,1,0:T(8,128)S(1)}, u32[]{:S(2)}, u32[]{:S(2)}) collective-permute-start(f32[2,16,256]{2,1,0:T(8,128)S(1)} %fusion.2), channel_id=1, source_target_pairs={{0,1},{1,0},{2,3},{3,2},{4,5},{5,4},{6,7},{7,6},{8,9},{9,8},{10,11... | collective-permute-start | bytes 98312 | tf_op jit(solution)/shard_map/ppermute | solution.py:25
  40.3 2.9 %layer_two.1 = bf16[8,128,256]{2,1,0:T(8,128)(2,1)} custom-call(s32[480]{0:T(512)S(1)} %get-tuple-element.17.table, bf16[68,256,128]{2,1,0:T(8,128)(2,1)S(1)} %get-tuple-element.27.h_ref, bf16[8,8,128,128]{3,2,1,0:T(8,128)(2,1)S(1)} %get-tuple-element.28.adj_two, bf16[2,256,256]{2,1,0:T(8,128)(2,1)S(1)} %get-tuple-element.29.w_ref), custom_call_target="tpu_custom_call" | custom-call | flops 536870912 | bytes 8388608 | tf_op jit(solution)/shard_map/layer_two/pallas_call | solution.py:334
  43.3 0.0 collective-permute-done.13
  43.3 0.5 %collective-permute-done.12 = f32[2,16,256]{2,1,0:T(8,128)S(1)} collective-permute-done((f32[2,16,256]{2,1,0:T(8,128)S(1)}, f32[2,16,256]{2,1,0:T(8,128)S(1)}, u32[]{:S(2)}, u32[]{:S(2)}) %collective-permute-start.12) | collective-permute-done | bytes 32800 | tf_op jit(solution)/shard_map/ppermute | solution.py:25
  43.8 0.0 collective-permute-done.11
  43.8 0.6 %add_add_fusion = f32[2,16,256]{2,1,0:T(8,128)} fusion(f32[2,16,256]{2,1,0:T(8,128)S(1)} %collective-permute-done.12, f32[2,16,256]{2,1,0:T(8,128)S(1)} %collective-permute-done.13, f32[2,16,256]{2,1,0:T(8,128)S(1)} %fusion.2, f32[2,16,256]{2,1,0:T(8,128)S(1)} %collective-permute-done.11), kind=kLoop, calls=%fused_computation.9 | loop fusion | flops 24576 | bytes 163840 | tf_op jit(solution)/shard_map/add | solution.py:401
  (3 shorter events, 0.0 us)
Async XLA Ops:
  2.3 12.3 %collective-permute-start.2 = (bf16[16,8704]{1,0:T(8,128)(2,1)S(1)}, bf16[16,8704]{1,0:T(8,128)(2,1)S(1)}, u32[]{:S(2)}, u32[]{:S(2)}) collective-permute-start(bf16[16,8704]{1,0:T(8,128)(2,1)S(1)} %pad_maximum_fusion.refs_0_), channel_id=1, source_target_pairs={{0,16},{4,20},{8,24},{12,28},{16,0},{20,4},{24,8},{28,12},{1,17},{... | collective-permute-start | bytes 835592 | tf_op jit(solution)/shard_map/ppermute | solution.py:25
  5.3 9.6 %collective-permute-start.1 = (bf16[16,8704]{1,0:T(8,128)(2,1)S(1)}, bf16[16,8704]{1,0:T(8,128)(2,1)S(1)}, u32[]{:S(2)}, u32[]{:S(2)}) collective-permute-start(bf16[16,8704]{1,0:T(8,128)(2,1)S(1)} %pad_maximum_fusion.refs_0_), channel_id=1, source_target_pairs={{0,8},{4,12},{8,0},{12,4},{16,24},{20,28},{24,16},{28,20},{1,9},{5... | collective-permute-start | bytes 835592 | tf_op jit(solution)/shard_map/ppermute | solution.py:25
  6.8 12.4 %collective-permute-start.3 = (bf16[16,8704]{1,0:T(8,128)(2,1)S(1)}, bf16[16,8704]{1,0:T(8,128)(2,1)S(1)}, u32[]{:S(2)}, u32[]{:S(2)}) collective-permute-start(bf16[16,8704]{1,0:T(8,128)(2,1)S(1)} %pad_maximum_fusion.refs_0_), channel_id=1, source_target_pairs={{0,24},{4,28},{8,16},{12,20},{16,8},{20,12},{24,0},{28,4},{1,25},{... | collective-permute-start | bytes 835592 | tf_op jit(solution)/shard_map/ppermute | solution.py:25
  14.9 4.3 %collective-permute-start.4 = (bf16[16,8704]{1,0:T(8,128)(2,1)S(1)}, bf16[16,8704]{1,0:T(8,128)(2,1)S(1)}, u32[]{:S(2)}, u32[]{:S(2)}) collective-permute-start(bf16[16,8704]{1,0:T(8,128)(2,1)S(1)} %collective-permute-done.1.refs_2_), channel_id=1, source_target_pairs={{0,4},{4,0},{8,12},{12,8},{16,20},{20,16},{24,28},{28,24},{1,5},{5... | collective-permute-start | bytes 835592 | tf_op jit(solution)/shard_map/ppermute | solution.py:25
  14.9 4.3 %collective-permute-start.5 = (bf16[16,8704]{1,0:T(8,128)(2,1)S(1)}, bf16[16,8704]{1,0:T(8,128)(2,1)S(1)}, u32[]{:S(2)}, u32[]{:S(2)}) collective-permute-start(bf16[16,8704]{1,0:T(8,128)(2,1)S(1)} %collective-permute-done.2.refs_4_), channel_id=1, source_target_pairs={{0,4},{4,0},{8,12},{12,8},{16,20},{20,16},{24,28},{28,24},{1,5},{5... | collective-permute-start | bytes 835592 | tf_op jit(solution)/shard_map/ppermute | solution.py:25
  15.4 3.8 %collective-permute-start = (bf16[16,8704]{1,0:T(8,128)(2,1)S(1)}, bf16[16,8704]{1,0:T(8,128)(2,1)S(1)}, u32[]{:S(2)}, u32[]{:S(2)}) collective-permute-start(bf16[16,8704]{1,0:T(8,128)(2,1)S(1)} %pad_maximum_fusion.refs_0_), channel_id=1, source_target_pairs={{0,4},{4,0},{8,12},{12,8},{16,20},{20,16},{24,28},{28,24},{1,5},{5... | collective-permute-start | bytes 835592 | tf_op jit(solution)/shard_map/ppermute | solution.py:25
  19.2 1.6 %collective-permute-start.6 = (bf16[16,8704]{1,0:T(8,128)(2,1)S(1)}, bf16[16,8704]{1,0:T(8,128)(2,1)S(1)}, u32[]{:S(2)}, u32[]{:S(2)}) collective-permute-start(bf16[16,8704]{1,0:T(8,128)(2,1)S(1)} %collective-permute-done.3.refs_6_), channel_id=1, source_target_pairs={{0,4},{4,0},{8,12},{12,8},{16,20},{20,16},{24,28},{28,24},{1,5},{5... | collective-permute-start | bytes 835592 | tf_op jit(solution)/shard_map/ppermute | solution.py:25
  27.1 1.3 %collective-permute-start.7 = (bf16[4,2,16,256]{3,2,1,0:T(8,128)(2,1)S(1)}, bf16[4,2,16,256]{3,2,1,0:T(8,128)(2,1)S(1)}, u32[]{:S(2)}, u32[]{:S(2)}) collective-permute-start(bf16[4,2,16,256]{3,2,1,0:T(8,128)(2,1)S(1)} %get-tuple-element.31), channel_id=1, source_target_pairs={{0,4},{4,0},{8,12},{12,8},{16,20},{20,16},{24,28},{28,24},{1,5},{5... | collective-permute-start | bytes 196616 | tf_op jit(solution)/shard_map/ppermute | solution.py:25
  28.5 4.0 %collective-permute-start.8 = (f32[2,16,256]{2,1,0:T(8,128)S(1)}, f32[2,16,256]{2,1,0:T(8,128)S(1)}, u32[]{:S(2)}, u32[]{:S(2)}) collective-permute-start(f32[2,16,256]{2,1,0:T(8,128)S(1)} %get-tuple-element.32), channel_id=1, source_target_pairs={{0,8},{4,12},{8,0},{12,4},{16,24},{20,28},{24,16},{28,20},{1,9},{5... | collective-permute-start | bytes 98312 | tf_op jit(solution)/shard_map/ppermute | solution.py:25
  30.0 4.9 %collective-permute-start.10 = (f32[2,16,256]{2,1,0:T(8,128)S(1)}, f32[2,16,256]{2,1,0:T(8,128)S(1)}, u32[]{:S(2)}, u32[]{:S(2)}) collective-permute-start(f32[2,16,256]{2,1,0:T(8,128)S(1)} %get-tuple-element.33), channel_id=1, source_target_pairs={{0,24},{4,28},{8,16},{12,20},{16,8},{20,12},{24,0},{28,4},{1,25},{... | collective-permute-start | bytes 98312 | tf_op jit(solution)/shard_map/ppermute | solution.py:25
  31.9 3.9 %collective-permute-start.9 = (f32[2,16,256]{2,1,0:T(8,128)S(1)}, f32[2,16,256]{2,1,0:T(8,128)S(1)}, u32[]{:S(2)}, u32[]{:S(2)}) collective-permute-start(f32[2,16,256]{2,1,0:T(8,128)S(1)} %get-tuple-element.34), channel_id=1, source_target_pairs={{0,16},{4,20},{8,24},{12,28},{16,0},{20,4},{24,8},{28,12},{1,17},{... | collective-permute-start | bytes 98312 | tf_op jit(solution)/shard_map/ppermute | solution.py:25
  35.9 7.4 %collective-permute-start.13 = (f32[2,16,256]{2,1,0:T(8,128)S(1)}, f32[2,16,256]{2,1,0:T(8,128)S(1)}, u32[]{:S(2)}, u32[]{:S(2)}) collective-permute-start(f32[2,16,256]{2,1,0:T(8,128)S(1)} %fusion.2), channel_id=1, source_target_pairs={{0,3},{1,2},{2,1},{3,0},{4,7},{5,6},{6,5},{7,4},{8,11},{9,10},{10,... | collective-permute-start | bytes 98312 | tf_op jit(solution)/shard_map/ppermute | solution.py:25
  38.9 4.8 %collective-permute-start.12 = (f32[2,16,256]{2,1,0:T(8,128)S(1)}, f32[2,16,256]{2,1,0:T(8,128)S(1)}, u32[]{:S(2)}, u32[]{:S(2)}) collective-permute-start(f32[2,16,256]{2,1,0:T(8,128)S(1)} %fusion.2), channel_id=1, source_target_pairs={{0,2},{1,3},{2,0},{3,1},{4,6},{5,7},{6,4},{7,5},{8,10},{9,11},{10,... | collective-permute-start | bytes 98312 | tf_op jit(solution)/shard_map/ppermute | solution.py:25
  38.9 4.8 %collective-permute-start.11 = (f32[2,16,256]{2,1,0:T(8,128)S(1)}, f32[2,16,256]{2,1,0:T(8,128)S(1)}, u32[]{:S(2)}, u32[]{:S(2)}) collective-permute-start(f32[2,16,256]{2,1,0:T(8,128)S(1)} %fusion.2), channel_id=1, source_target_pairs={{0,1},{1,0},{2,3},{3,2},{4,5},{5,4},{6,7},{7,6},{8,9},{9,8},{10,11... | collective-permute-start | bytes 98312 | tf_op jit(solution)/shard_map/ppermute | solution.py:25
